TPU v7x, 32 devices: a whole 2x2x4 slice. The times are simulated.
32 devices in a mesh: dp: 8 (over z, x), tensor: 4 (over y, core).
Axes of the slice: x: 2, y: 2, z: 4, core: 2. Of those that a mesh axis runs over, the one named last changes fastest.
Arguments:
- tokens: bfloat16 [8192, 2048], P('dp', 'tensor'), may hold values from -6 to 6
- cotangent: bfloat16 [8192, 2048], P('dp', 'tensor'), may hold values from -6 to 6
- lengths: int32 [8], P('dp'), may hold values from 256 to 1024, as said below
- gains: float32 [4, 2048], P(None, 'tensor')
- gain_stats: float32 [4, 2048], P(None, 'tensor'), may hold values from 2048 to 8192
- gain_roots: float32 [4, 2048], P(None, 'tensor'), may hold values from 0.0055242716 to 0.022097087
- master: float32 [4, 1024, 128, 128], P('tensor', 'dp'), may hold values from -0.125 to 0.125
- block_order: int32 [4, 1024], P('tensor'), may hold values from 0 to 1023, each once within a row
- left_stats: float32 [4, 1024, 128, 128], P('tensor', 'dp')
- right_stats: float32 [4, 1024, 128, 128], P('tensor', 'dp')
- left_roots: float32 [4, 1024, 128, 128], P('tensor', 'dp')
- right_roots: float32 [4, 1024, 128, 128], P('tensor', 'dp')
Outputs:
- block_out: bfloat16 [8192, 2048], P('dp', 'tensor')
- token_grads: bfloat16 [8192, 2048], P('dp', 'tensor')
- block_grads: float32 [4, 1024, 128, 128], P('tensor', 'dp')
- left_new: float32 [4, 1024, 128, 128], P('tensor', 'dp')
- right_new: float32 [4, 1024, 128, 128], P('tensor', 'dp')
- master_new: float32 [4, 1024, 128, 128], P('tensor', 'dp')
- gain_grads: float32 [4, 2048], P(None, 'tensor')
- gain_stats_new: float32 [4, 2048], P(None, 'tensor')
- gains_new: float32 [4, 2048], P(None, 'tensor')
Inputs may be any that keep to these rules, and one draw needn't show every extreme that they name: `lengths`: one sequence of the draw has exactly 1024 tokens. `block_order`: each row names every block of its tensor shard once.
All inputs are finite; a program needn't handle non-finite values.
Results may differ from a plain program's by a relative error of at most 0.024.
The roundings to bfloat16 on the way count: a program that leaves them out, or rounds other values in their place, can miss the bound.
Values may be sent and summed in bfloat16 or wider, within the bound.
No kernel may reach another device: no remote copies, remote signals or barrier semaphores. Data moves between devices by JAX's collectives and lax.ppermute only.
A program may use at most 384 MiB of HBM per device.

v0:
```python
import jax
import jax.numpy as jnp
from jax import lax
from jax.sharding import PartitionSpec as P

HEADS = 16
HD = 128
FF = 8192


EPSILON = 1e-06
THETA = 500000.0
DECAY = 0.5
LEARN_RATE = 0.25
GAIN_RATE = 0.2
HIGHEST_PREC = lax.Precision.HIGHEST


def from_blocks(blocks, row_count, col_count, size_b):
    return (
        blocks.reshape(row_count // size_b, col_count // size_b, size_b, size_b)
        .transpose(0, 2, 1, 3)
        .reshape(row_count, col_count)
    )


def to_blocks(matrix, size_b):
    row_count, col_count = matrix.shape
    return (
        matrix.reshape(row_count // size_b, size_b, col_count // size_b, size_b)
        .transpose(0, 2, 1, 3)
        .reshape(-1, size_b, size_b)
    )


def split_stack(stack, width_d, hidden_local, width_local, size_b):
    shapes = (
        [(width_d, width_local)] * 3
        + [(width_local, width_d)]
        + [(width_d, hidden_local)] * 2
        + [(hidden_local, width_d)]
    )
    matrices = []
    offset = 0
    for row_count, col_count in shapes:
        count_b = row_count // size_b * (col_count // size_b)
        matrices.append(from_blocks(stack[offset : offset + count_b], row_count, col_count, size_b))
        offset = offset + count_b
    return matrices


def rope_tables(seq_len, head_dim):
    half_dim = head_dim // 2
    freqs = THETA ** (-(2.0 * jnp.arange(half_dim, dtype=jnp.float32)) / head_dim)
    angles = jnp.arange(seq_len, dtype=jnp.float32)[:, None] * freqs[None, :]
    return (jnp.cos(angles)[:, None, :], jnp.sin(angles)[:, None, :])


def rotary(values, cos_t, sin_t):
    half_dim = values.shape[-1] // 2
    first_half = values[..., :half_dim]
    second_half = values[..., half_dim:]
    return jnp.concatenate(
        [first_half * cos_t - second_half * sin_t, second_half * cos_t + first_half * sin_t],
        axis=-1,
    )


def body(
    tokens,
    cotangent,
    lengths,
    gains,
    gain_stats,
    gain_roots,
    master,
    block_order,
    left_stats,
    right_stats,
    left_roots,
    right_roots,
):
    f32 = jnp.float32
    bf16 = jnp.bfloat16
    tensor_count = lax.axis_size("tensor")
    col_start = lax.axis_index("tensor") * tokens.shape[1]
    width_local = tokens.shape[1]
    width_d = width_local * tensor_count
    hidden_local = FF // tensor_count
    heads_local = HEADS // tensor_count
    size_b = master.shape[-1]
    slot_count = lengths.shape[0]
    tok_rows = tokens.shape[0]
    slot_len = tok_rows // slot_count
    score_scale = HD ** (-0.5)
    gathered = lax.all_gather(master.astype(bf16), "dp", axis=1, tiled=True)[0]
    slot_order = block_order[0]
    local_stack = jnp.zeros_like(gathered).at[slot_order].set(gathered)
    proj_q, proj_k, proj_v, proj_o, proj_gate, proj_up, proj_down = split_stack(
        local_stack, width_d, hidden_local, width_local, size_b
    )
    gains_low = gains.astype(bf16)
    gain_local = gains_low.astype(f32)
    tok_full = lax.all_gather(tokens, "tensor", axis=1, tiled=True)
    positions = jnp.arange(slot_len)
    live_rows = (positions[None, :] < lengths[:, None]).astype(f32).reshape(tok_rows)
    cos_t, sin_t = rope_tables(slot_len, HD)
    head_shape = (slot_count, slot_len, heads_local, HD)
    queries = jnp.dot(tok_full, proj_q, preferred_element_type=f32)
    keys_raw = jnp.dot(tok_full, proj_k, preferred_element_type=f32)
    values_raw = jnp.dot(tok_full, proj_v, preferred_element_type=f32)
    sq_q, sq_k = lax.psum(
        (jnp.sum(queries * queries, axis=-1), jnp.sum(keys_raw * keys_raw, axis=-1)), "tensor"
    )
    scale_q = lax.rsqrt(sq_q / width_d + EPSILON)[:, None]
    scale_k = lax.rsqrt(sq_k / width_d + EPSILON)[:, None]
    q_low = rotary((queries * scale_q * gain_local[0]).reshape(head_shape), cos_t, sin_t).astype(
        bf16
    )
    k_low = rotary((keys_raw * scale_k * gain_local[1]).reshape(head_shape), cos_t, sin_t).astype(
        bf16
    )
    v_low = values_raw.astype(bf16).reshape(head_shape)
    scores = jnp.einsum("sqhd,skhd->shqk", q_low, k_low, preferred_element_type=f32) * score_scale
    causal = (positions[None, :] <= positions[:, None])[None, None]
    inside = positions[None, None, None, :] < lengths[:, None, None, None]
    scores = jnp.where(causal & inside, scores, -1e30)
    row_max = jnp.max(scores, axis=-1, keepdims=True)
    attn_probs = jnp.exp(scores - row_max)
    attn_probs = attn_probs / jnp.sum(attn_probs, axis=-1, keepdims=True)
    probs_low = attn_probs.astype(bf16)
    attn_vals = jnp.einsum("shqk,skhd->sqhd", probs_low, v_low, preferred_element_type=f32)
    attn_low = attn_vals.reshape(tok_rows, width_local).astype(bf16)
    attn_part = jnp.dot(attn_low, proj_o, preferred_element_type=f32)
    branch = lax.psum(attn_part.astype(jnp.bfloat16), "tensor").astype(jnp.float32)
    rms_a = lax.rsqrt(jnp.mean(branch * branch, axis=-1, keepdims=True) + EPSILON)
    cot_full, gains_all = (
        lax.all_gather(cotangent, "tensor", axis=1, tiled=True),
        lax.all_gather(gains_low, "tensor", axis=1, tiled=True),
    )
    gain_full = gains_all.astype(f32)
    hidden_state = tok_full.astype(f32) + branch * rms_a * gain_full[2]
    hidden_low = hidden_state.astype(bf16)
    gate_act = jnp.dot(hidden_low, proj_gate, preferred_element_type=f32)
    up_act = jnp.dot(hidden_low, proj_up, preferred_element_type=f32)
    sig_gate = jax.nn.sigmoid(gate_act)
    silu_act = gate_act * sig_gate
    inner_low = (silu_act * up_act).astype(bf16)
    mlp_part = jnp.dot(inner_low, proj_down, preferred_element_type=f32)
    mlp_out = lax.psum(mlp_part.astype(jnp.bfloat16), "tensor").astype(jnp.float32)
    rms_m = lax.rsqrt(jnp.mean(mlp_out * mlp_out, axis=-1, keepdims=True) + EPSILON)
    result = hidden_state + mlp_out * rms_m * gain_full[3]
    block_out = lax.dynamic_slice_in_dim(result, col_start, width_local, 1).astype(bf16)
    grad_out = cot_full.astype(f32) * live_rows[:, None]
    d_gain_m = lax.dynamic_slice_in_dim(
        jnp.sum(grad_out * mlp_out * rms_m, axis=0), col_start, width_local, 0
    )
    scaled_m = gain_full[3] * grad_out
    d_mlp = rms_m * scaled_m - mlp_out * rms_m**3 * jnp.mean(
        scaled_m * mlp_out, axis=-1, keepdims=True
    )
    d_mlp_low = d_mlp.astype(bf16)
    grad_down = jnp.einsum("tf,td->fd", inner_low, d_mlp_low, preferred_element_type=f32)
    d_inner = jnp.einsum("td,fd->tf", d_mlp_low, proj_down, preferred_element_type=f32)
    d_gate = (d_inner * up_act * sig_gate * (1.0 + gate_act * (1.0 - sig_gate))).astype(bf16)
    d_up = (d_inner * silu_act).astype(bf16)
    grad_gate = jnp.einsum("td,tf->df", hidden_low, d_gate, preferred_element_type=f32)
    grad_up = jnp.einsum("td,tf->df", hidden_low, d_up, preferred_element_type=f32)
    back_part = jnp.einsum("tf,df->td", d_gate, proj_gate, preferred_element_type=f32) + jnp.einsum(
        "tf,df->td", d_up, proj_up, preferred_element_type=f32
    )
    d_hidden = grad_out + lax.psum(back_part.astype(jnp.bfloat16), "tensor").astype(jnp.float32)
    d_gain_a = lax.dynamic_slice_in_dim(
        jnp.sum(d_hidden * branch * rms_a, axis=0), col_start, width_local, 0
    )
    scaled_a = gain_full[2] * d_hidden
    d_branch = rms_a * scaled_a - branch * rms_a**3 * jnp.mean(
        scaled_a * branch, axis=-1, keepdims=True
    )
    d_branch_low = d_branch.astype(bf16)
    d_hidden_loc = lax.dynamic_slice_in_dim(d_hidden, col_start, width_local, 1)
    grad_o = jnp.einsum("tk,td->kd", attn_low, d_branch_low, preferred_element_type=f32)
    d_attn = (
        jnp.einsum("td,kd->tk", d_branch_low, proj_o, preferred_element_type=f32)
        .astype(bf16)
        .reshape(head_shape)
    )
    d_probs = jnp.einsum("sqhd,skhd->shqk", d_attn, v_low, preferred_element_type=f32)
    row_delta = jnp.sum(attn_probs * d_probs, axis=-1, keepdims=True)
    d_scores = (attn_probs * (d_probs - row_delta)).astype(bf16)
    d_qrot = (
        jnp.einsum("shqk,skhd->sqhd", d_scores, k_low, preferred_element_type=f32) * score_scale
    )
    d_krot = (
        jnp.einsum("shqk,sqhd->skhd", d_scores, q_low, preferred_element_type=f32) * score_scale
    )
    d_values = (
        jnp.einsum("shqk,sqhd->skhd", probs_low, d_attn, preferred_element_type=f32)
        .astype(bf16)
        .reshape(tok_rows, width_local)
    )
    d_qn = rotary(d_qrot, cos_t, -sin_t).reshape(tok_rows, width_local)
    d_kn = rotary(d_krot, cos_t, -sin_t).reshape(tok_rows, width_local)
    d_gain_q = jnp.sum(d_qn * queries * scale_q, axis=0)
    d_gain_k = jnp.sum(d_kn * keys_raw * scale_k, axis=0)
    scaled_q = gain_local[0] * d_qn
    scaled_k = gain_local[1] * d_kn
    stat_q, stat_k = lax.psum(
        (jnp.sum(scaled_q * queries, axis=-1), jnp.sum(scaled_k * keys_raw, axis=-1)), "tensor"
    )
    d_queries = (scale_q * scaled_q - queries * scale_q**3 * (stat_q / width_d)[:, None]).astype(
        bf16
    )
    d_keys = (scale_k * scaled_k - keys_raw * scale_k**3 * (stat_k / width_d)[:, None]).astype(bf16)
    grad_q = jnp.einsum("td,tk->dk", tok_full, d_queries, preferred_element_type=f32)
    grad_k = jnp.einsum("td,tk->dk", tok_full, d_keys, preferred_element_type=f32)
    grad_v = jnp.einsum("td,tk->dk", tok_full, d_values, preferred_element_type=f32)
    input_part = jnp.einsum("tk,dk->td", d_queries, proj_q, preferred_element_type=f32)
    input_part = input_part + jnp.einsum("tk,dk->td", d_keys, proj_k, preferred_element_type=f32)
    input_part = input_part + jnp.einsum("tk,dk->td", d_values, proj_v, preferred_element_type=f32)
    token_grads = (
        lax.psum_scatter(
            input_part.astype(jnp.bfloat16), "tensor", scatter_dimension=1, tiled=True
        ).astype(jnp.float32)
        + d_hidden_loc
    ).astype(bf16)
    gain_terms = jnp.stack([d_gain_q, d_gain_k, d_gain_a, d_gain_m], axis=0)
    gain_grads = lax.psum(gain_terms, "dp")
    gain_stats_new = DECAY * gain_stats + (1.0 - DECAY) * gain_grads * gain_grads
    gains_new = gains - GAIN_RATE * gain_grads * gain_roots
    grad_stack = jnp.concatenate(
        [
            to_blocks(matrix, size_b)
            for matrix in [grad_q, grad_k, grad_v, grad_o, grad_gate, grad_up, grad_down]
        ],
        axis=0,
    )
    block_grads = lax.psum_scatter(
        grad_stack[slot_order].astype(jnp.bfloat16), "dp", scatter_dimension=0, tiled=True
    ).astype(jnp.float32)[None]
    left_new = DECAY * left_stats + (1.0 - DECAY) * jnp.einsum(
        "tbij,tbkj->tbik", block_grads, block_grads, precision=HIGHEST_PREC
    )
    right_new = DECAY * right_stats + (1.0 - DECAY) * jnp.einsum(
        "tbji,tbjk->tbik", block_grads, block_grads, precision=HIGHEST_PREC
    )
    left_part = jnp.einsum("tbij,tbjk->tbik", left_roots, block_grads, precision=HIGHEST_PREC)
    precond = jnp.einsum("tbij,tbjk->tbik", left_part, right_roots, precision=HIGHEST_PREC)
    master_new = master - LEARN_RATE * precond
    return (
        block_out,
        token_grads,
        block_grads,
        left_new,
        right_new,
        master_new,
        gain_grads,
        gain_stats_new,
        gains_new,
    )


def solution(mesh):
    placed = (
        P("dp", "tensor"),
        P("dp", "tensor"),
        P("dp"),
        P(None, "tensor"),
        P(None, "tensor"),
        P(None, "tensor"),
        P("tensor", "dp", None, None),
        P("tensor", None),
        P("tensor", "dp", None, None),
        P("tensor", "dp", None, None),
        P("tensor", "dp", None, None),
        P("tensor", "dp", None, None),
    )
    return jax.shard_map(
        body,
        mesh=mesh,
        in_specs=placed,
        out_specs=(
            P("dp", "tensor"),
            P("dp", "tensor"),
            P("tensor", "dp", None, None),
            P("tensor", "dp", None, None),
            P("tensor", "dp", None, None),
            P("tensor", "dp", None, None),
            P(None, "tensor"),
            P(None, "tensor"),
            P(None, "tensor"),
        ),
        check_vma=False,
    )
```

profile of v0, /device:TPU:0, one launch (start us, length us, event | category | flops | bytes accessed | tf_op | source)
XLA Modules:
  0.0 2170.6 jit_solution(10639803921115132765)
XLA Ops:
  25.5 628.8 %all-gather.6.cloned.1.call-done = bf16[1,1024,128,128]{3,2,0,1:T(8,128)(2,1)} async-done(((bf16[1,128,128,128]{3,2,0,1:T(8,128)(2,1)}), bf16[1,1024,128,128]{3,2,0,1:T(8,128)(2,1)}) %all-gather.6.cloned.1.call-update) | async-done | bytes 33554448 | tf_op jit(solution)/shard_map/all_gather | solution.py:96
  654.2 12.2 broadcast_in_dim.15
  666.4 149.2 %scatter_fusion = bf16[1024,128,128]{2,1,0:T(8,128)(2,1)} fusion(bf16[1024,128,128]{2,1,0:T(8,128)(2,1)} %broadcast_in_dim.15, s32[1024]{0:T(1024)S(1)} %bitcast.382, bf16[1024,128,128]{2,1,0:T(8,128)(2,1)} %bitcast.324), kind=kCustom, calls=%fused_computation.1 | custom fusion | bytes 100667392 | tf_op jit(solution)/shard_map/scatter | solution.py:98
  875.5 12.8 fusion.127
  905.9 17.4 fusion.121
  923.3 13.9 copy.106
  937.3 14.2 copy.107
  951.4 14.3 copy.108
  965.7 24.8 %all-reduce.6.cloned.1.call-done = bf16[1024,2048]{1,0:T(8,128)(2,1)} async-done(((bf16[1024,2048]{1,0:T(8,128)(2,1)}), bf16[1024,2048]{1,0:T(8,128)(2,1)}) %all-reduce.6.cloned.1.call-update) | async-done | bytes 4194320 | tf_op jit(solution)/shard_map/psum | solution.py:135
  1013.0 16.0 multiply_convert_fusion.3
  1029.0 12.2 fusion.45
  1041.9 85.1 %all-reduce.8.cloned.1.call-done = bf16[1024,2048]{1,0:T(8,128)(2,1)} async-done(((bf16[1024,2048]{1,0:T(8,128)(2,1)}), bf16[1024,2048]{1,0:T(8,128)(2,1)}) %all-reduce.8.cloned.1.call-update) | async-done | bytes 4194320 | tf_op jit(solution)/shard_map/psum | solution.py:150
  1130.1 33.0 %all-gather.8.cloned.1.call-done = bf16[1024,2048]{1,0:T(8,128)(2,1)} async-done(((bf16[1024,512]{1,0:T(8,128)(2,1)}), bf16[1024,2048]{1,0:T(8,128)(2,1)}) %all-gather.8.cloned.1.call-update) | async-done | bytes 4194320 | tf_op jit(solution)/shard_map/all_gather | solution.py:138
  1169.2 21.2 multiply_convert_fusion.2
  1190.4 12.8 fusion.15
  1203.2 12.8 add_convert_fusion.1
  1217.3 14.4 convolution_bitcast_fusion.2
  1251.1 50.6 %all-reduce.10.cloned.1.call-done = bf16[1024,2048]{1,0:T(8,128)(2,1)} async-done(((bf16[1024,2048]{1,0:T(8,128)(2,1)}), bf16[1024,2048]{1,0:T(8,128)(2,1)}) %all-reduce.10.cloned.1.call-update) | async-done | bytes 4194320 | tf_op jit(solution)/shard_map/psum | solution.py:172
  1396.1 14.0 convolution_bitcast_fusion.1
  1429.5 15.4 convolution_bitcast_fusion
  1542.4 36.1 %gather_fusion = bf16[1024,128,128]{2,1,0:T(8,128)(2,1)} fusion(bf16[1024,128,128]{2,1,0:T(8,128)(2,1)} %constant_dynamic-update-slice_fusion, s32[1024]{0:T(1024)S(1)} %copy-done.60), kind=kCustom, calls=%fused_computation | custom fusion | bytes 67112960 | tf_op jit(solution)/shard_map/gather | solution.py:239
  1586.4 23.1 %psum.63 = f32[4,512]{1,0:T(4,128)S(1)} all-reduce(f32[4,512]{1,0:T(4,128)S(1)} %pad_maximum_fusion.4), channel_id=1, replica_groups=mesh['dp'=8,'tensor'=4] {'dp'}, use_global_device_ids=true, to_apply=%region_25.26 | all-reduce | flops 2048 | bytes 16384 | tf_op jit(solution)/shard_map/psum | solution.py:228
  1613.4 509.6 %reduce-scatter.5.cloned.1.call-done = bf16[128,128,128]{2,1,0:T(8,128)(2,1)} async-done(((bf16[1024,128,128]{2,1,0:T(8,128)(2,1)}), bf16[128,128,128]{2,1,0:T(8,128)(2,1)}) %reduce-scatter.5.cloned.1.call-update) | async-done | bytes 4194320 | tf_op jit(solution)/shard_map/reduce_scatter | solution.py:238
  2130.1 14.0 bitcast_subtract_fusion
  (302 shorter events, 396.9 us)
Async XLA Ops:
  7.2 647.0 %all-gather.6.cloned.1.call-start = ((), (), s32[]{:S(2)}) async-start(), calls=%async_computation.3 | async-start | bytes 37748736 | tf_op jit(solution)/shard_map/all_gather | solution.py:96
  13.6 819.5 %all-gather.4.cloned.1.call-start = ((), (), s32[]{:S(2)}) async-start(), calls=%async_computation.2 | async-start | bytes 5242880 | tf_op jit(solution)/shard_map/all_gather | solution.py:104
  14.4 976.2 %all-reduce.6.cloned.1.call-start = ((), (), s32[]{:S(2)}) async-start(), calls=%async_computation.4 | async-start | bytes 8388608 | tf_op jit(solution)/shard_map/psum | solution.py:135
  21.4 829.0 %copy-start.53 = (f32[1,512]{1,0:T(1,128)}, f32[1,512]{1,0:T(1,128)S(1)}, u32[]{:S(2)}) copy-start(f32[1,512]{1,0:T(1,128)S(1)} %get-tuple-element.61) | copy-start | bytes 6148
  21.4 838.6 %copy-start.51 = (f32[1,512]{1,0:T(1,128)}, f32[1,512]{1,0:T(1,128)S(1)}, u32[]{:S(2)}) copy-start(f32[1,512]{1,0:T(1,128)S(1)} %get-tuple-element.62) | copy-start | bytes 6148
  21.4 645.0 %copy-start.47 = (s32[1024,1]{0,1:T(1,128)}, s32[1024,1]{0,1:T(1,128)S(1)}, u32[]{:S(2)}) copy-start(s32[1024,1]{0,1:T(1,128)S(1)} %compare_select_fusion) | copy-start | bytes 12292
  24.1 846.9 %copy-start.19 = (f32[1024,64]{1,0:T(8,128)}, f32[1024,64]{1,0:T(8,128)S(1)}, u32[]{:S(2)}) copy-start(f32[1024,64]{1,0:T(8,128)S(1)} %get-tuple-element.65) | copy-start | bytes 786436
  905.8 221.2 %all-reduce.8.cloned.1.call-start = ((), (), s32[]{:S(2)}) async-start(), calls=%async_computation.5 | async-start | bytes 8388608 | tf_op jit(solution)/shard_map/psum | solution.py:150
  905.9 88.5 %copy-start.37 = (f32[1,2048]{1,0:T(1,128)}, f32[1,2048]{1,0:T(1,128)S(1)}, u32[]{:S(2)}) copy-start(f32[1,2048]{1,0:T(1,128)S(1)} %get-tuple-element.50) | copy-start | bytes 24580
  905.9 263.3 %copy-start.45 = (f32[1,2048]{1,0:T(1,128)}, f32[1,2048]{1,0:T(1,128)S(1)}, u32[]{:S(2)}) copy-start(f32[1,2048]{1,0:T(1,128)S(1)} %get-tuple-element.49) | copy-start | bytes 24580
  1001.4 27.6 %slice-start.10 = ((s8[8388608]{0:T(1024)(128)(4,1)}), s8[4194304]{0:T(1024)(128)(4,1)S(1)}, s32[]{:S(2)}) async-start(s8[8388608]{0:T(1024)(128)(4,1)} %bitcast.350), calls=%async_computation.20 | async-start | bytes 8388608
  1041.2 121.8 %all-gather.8.cloned.1.call-start = ((), (), s32[]{:S(2)}) async-start(), calls=%async_computation.6 | async-start | bytes 5242880 | tf_op jit(solution)/shard_map/all_gather | solution.py:138
  1041.8 259.8 %all-reduce.10.cloned.1.call-start = ((), (), s32[]{:S(2)}) async-start(), calls=%async_computation.7 | async-start | bytes 8388608 | tf_op jit(solution)/shard_map/psum | solution.py:172
  1130.1 39.1 %copy-start.49 = (f32[1024]{0:T(1024)}, f32[1024]{0:T(1024)S(1)}, u32[]{:S(2)}) copy-start(f32[1024]{0:T(1024)S(1)} %get-tuple-element.60) | copy-start | bytes 12292
  1130.1 39.1 %copy-start.67 = (f32[1024]{0:T(1024)}, f32[1024]{0:T(1024)S(1)}, u32[]{:S(2)}) copy-start(f32[1024]{0:T(1024)S(1)} %get-tuple-element.59) | copy-start | bytes 12292
  1216.0 394.1 %reduce-scatter.3.cloned.1.call-start = ((), (), s32[]{:S(2)}) async-start(), calls=%async_computation.8 | async-start | bytes 5242880 | tf_op jit(solution)/shard_map/reduce_scatter | solution.py:222
  1241.7 60.0 %copy-start.38 = (f32[1,2048]{1,0:T(1,128)S(1)}, f32[1,2048]{1,0:T(1,128)}, u32[]{:S(2)}) copy-start(f32[1,2048]{1,0:T(1,128)} %copy-done.37) | copy-start | bytes 24580
  1241.7 60.0 %copy-start.44 = (f32[1024]{0:T(1024)S(1)}, f32[1024]{0:T(1024)}, u32[]{:S(2)}) copy-start(f32[1024]{0:T(1024)} %copy-done.43) | copy-start | bytes 12292
  1251.1 58.8 %copy-start.63 = (f32[1024]{0:T(1024)S(1)}, f32[1024]{0:T(1024)}, u32[]{:S(2)}) copy-start(f32[1024]{0:T(1024)} %get-tuple-element.57) | copy-start | bytes 12292
  1395.7 727.3 %reduce-scatter.5.cloned.1.call-start = ((), (), s32[]{:S(2)}) async-start(), calls=%async_computation.9 | async-start | bytes 37748736 | tf_op jit(solution)/shard_map/reduce_scatter | solution.py:238
  1582.6 26.9 %copy-start.56 = (f32[4,512]{1,0:T(4,128)S(1)}, f32[4,512]{1,0:T(4,128)}, u32[]{:S(2)}) copy-start(f32[4,512]{1,0:T(4,128)} %param.15) | copy-start | bytes 24580
  1582.6 26.9 %copy-start.65 = (f32[4,512]{1,0:T(4,128)S(1)}, f32[4,512]{1,0:T(4,128)}, u32[]{:S(2)}) copy-start(f32[4,512]{1,0:T(4,128)} %param.17) | copy-start | bytes 24580
  1582.6 26.9 %copy-start.66 = (f32[4,512]{1,0:T(4,128)S(1)}, f32[4,512]{1,0:T(4,128)}, u32[]{:S(2)}) copy-start(f32[4,512]{1,0:T(4,128)} %param.16) | copy-start | bytes 24580
  1609.5 520.6 %copy-start.57 = (f32[4,512]{1,0:T(4,128)}, f32[4,512]{1,0:T(4,128)S(1)}, u32[]{:S(2)}) copy-start(f32[4,512]{1,0:T(4,128)S(1)} %psum.63) | copy-start | bytes 24580
  (73 other events, 539.6 us)
Sparse Core Ops, SparseCore 0:
  13.8 640.4 all-gather.5
  655.8 34.4 all-gather.3
  906.0 84.5 all-reduce.5
  1041.3 85.6 all-reduce.7
  1128.4 34.6 all-gather.7
  1216.1 85.4 all-reduce.9
  1395.8 45.0 reduce-scatter.2
  1578.6 544.3 reduce-scatter.4
where the time goes:
time: 2180 us; the launch traced here: 2170 us
  waiting for transfers between devices  1330 us (61%)
  local copies, waits for them, and re-layouts  427 us (20%)
  matrix products  260 us (12%)
  other arithmetic  90.7 us (4%)
  blocking collectives  42.9 us (2%)
    all_gather x1, waiting for transfers between devices, body(): gathered = lax.all_gather(master.astype(bf16), 'dp', axis=1, tiled=True)[0]  629 us
    reduce_scatter x1, waiting for transfers between devices, body(): lax.psum_scatter(grad_stack[slot_order].astype(jnp.bfloat16), 'dp', scatt...  510 us
    scatter x1, local copies, waits for them, and re-layouts, body(): local_stack = jnp.zeros_like(gathered).at[slot_order].set(gathered)  149 us
    psum x1, waiting for transfers between devices, body(): lax.psum(mlp_part.astype(jnp.bfloat16), 'tensor').astype(jnp.float32)  85.1 us
    unnamed x194, local copies, waits for them, and re-layouts  80.8 us
    transpose x7, local copies, waits for them, and re-layouts, from_blocks(): return blocks.reshape(row_count // size_b, col_count // size_b, size_b, s...  58.8 us
    psum x1, waiting for transfers between devices, body(): lax.psum(back_part.astype(jnp.bfloat16), 'tensor').astype(jnp.float32)  50.6 us
  transfers between devices with their start and end apart: 8, of which 6 were waited for; matrix products, arithmetic and copies ran while one was open for 22% of the time, Pallas kernels for 0%

commit v1 on v0

v1 whole, which is shorter than its diff:
```python
import jax
import jax.numpy as jnp
import numpy as np
from jax import lax
from jax.experimental import pallas as pl
from jax.experimental.pallas import tpu as pltpu
from jax.sharding import PartitionSpec as P

HEADS = 16
HD = 128
FF = 8192
EPSILON = 1e-06
THETA = 500000.0
DECAY = 0.5
LEARN_RATE = 0.25
GAIN_RATE = 0.2
NEG = -1e30
MIB = 1024 * 1024
f32 = jnp.float32
bf16 = jnp.bfloat16


def after(value, *others):
    return lax.optimization_barrier((value,) + others)[0]


class Links:
    def __init__(self):
        self.n_dp = lax.axis_size("dp")
        self.n_t = lax.axis_size("tensor")
        self.nz = self.n_dp // 2
        self.ny = self.n_t // 2
        self.d = lax.axis_index("dp")
        self.z, self.x = self.d // 2, self.d % 2
        self.t = lax.axis_index("tensor")
        self.y, self.c = self.t // 2, self.t % 2
        self.z_groups = [[2 * z + x for z in range(self.nz)] for x in range(2)]

    def ring(self, value):
        pairs = [(2 * z + x, 2 * ((z - 1) % self.nz) + x) for z in range(self.nz) for x in range(2)]
        return lax.ppermute(value, "dp", pairs)

    def gather_z(self, value):
        return lax.all_gather(value, "dp", axis=0, tiled=True, axis_index_groups=self.z_groups)

    def reduce_z(self, value):
        return lax.psum_scatter(
            value, "dp", scatter_dimension=0, tiled=True, axis_index_groups=self.z_groups
        )

    def swap_x(self, value):
        return lax.ppermute(value, "dp", [(i, i ^ 1) for i in range(self.n_dp)])

    def swap_core(self, value):
        return lax.ppermute(value, "tensor", [(i, i ^ 1) for i in range(self.n_t)])

    def shift_y(self, value, step):
        pairs = [(i, 2 * ((i // 2 + step) % self.ny) + i % 2) for i in range(self.n_t)]
        return lax.ppermute(value, "tensor", pairs)

    def shift_t(self, value, step):
        return lax.ppermute(value, "tensor", [(i, (i + step) % self.n_t) for i in range(self.n_t)])

    def gather_rows(self, own, meanwhile=None):
        rows = own.shape[0]
        pieces = [(self.y, own)]
        for step in range(1, self.ny):
            pieces.append(((self.y + self.ny - step) % self.ny, self.shift_y(own, step)))
        parts, places = [], []
        for row_y, piece in pieces:
            parts += [piece, self.swap_core(piece)]
            places += [2 * row_y + self.c, 2 * row_y + 1 - self.c]
        if meanwhile is not None:
            parts[-1] = after(parts[-1], *meanwhile(own))
        return stack_rows(parts, jnp.stack(places))

    def reduce_rows(self, part, meanwhile=None):
        rows = part.shape[0] // self.n_t
        cut = part.reshape((self.ny, 2, rows, part.shape[1]))
        got = self.swap_core(lax.dynamic_index_in_dim(cut, 1 - self.c, 1, False))
        kept = lax.dynamic_index_in_dim(cut, self.c, 1, False)
        both = (kept.astype(f32) + got.astype(f32)).astype(bf16)
        total = lax.dynamic_index_in_dim(both, self.y, 0, False).astype(f32)
        for step in range(1, self.ny):
            piece = lax.dynamic_index_in_dim(both, (self.y + step) % self.ny, 0, False)
            got = self.shift_y(piece, step)
            if meanwhile is not None and step == 1:
                got = after(got, *meanwhile(both))
            total = total + got.astype(f32)
        return total

    def rows_to_cols(self, own):
        rows, width = own.shape[0], own.shape[1] // self.n_t
        full = jnp.zeros((rows * self.n_t, width), own.dtype)
        for step in range(self.n_t):
            piece = lax.dynamic_slice_in_dim(own, ((self.t + step) % self.n_t) * width, width, 1)
            if step:
                piece = self.shift_t(piece, step)
            row0 = ((self.t + self.n_t - step) % self.n_t) * rows
            full = lax.dynamic_update_slice_in_dim(full, piece, row0, 0)
        return full


def fit(count, most=8):
    return next(step for step in (8, 4, 2, 1) if step <= most and count % step == 0)


def stack_rows(parts, places):
    rows, cols = parts[0].shape
    n = len(parts)

    def kernel(places_ref, *refs):
        out, sem = refs[n], refs[n + 1]
        copies = []
        for i in range(n):
            start = pl.multiple_of(places_ref[i] * rows, rows)
            copies.append(pltpu.make_async_copy(refs[i], out.at[pl.ds(start, rows), :], sem.at[i]))
            copies[-1].start()
        for copy in copies:
            copy.wait()

    return pl.pallas_call(
        kernel,
        grid_spec=pltpu.PrefetchScalarGridSpec(
            num_scalar_prefetch=1,
            grid=(1,),
            in_specs=[pl.BlockSpec(memory_space=pl.ANY)] * n,
            out_specs=pl.BlockSpec(memory_space=pltpu.VMEM),
            scratch_shapes=[pltpu.SemaphoreType.DMA((n,))],
        ),
        out_shape=jax.ShapeDtypeStruct((n * rows, cols), parts[0].dtype),
        compiler_params=pltpu.CompilerParams(vmem_limit_bytes=32 * MIB),
        name="stack_rows",
    )(places, *parts)


def sorted_tiles(master, perm, lo, hi):
    size_b = master.shape[-1]
    step = fit(hi - lo)

    def kernel(perm_ref, *refs):
        for j in range(step):
            refs[step][j] = refs[j][0].astype(bf16)

    def spec(j):
        return pl.BlockSpec((1, size_b, size_b), lambda i, p: (p[lo + step * i + j], 0, 0))

    return pl.pallas_call(
        kernel,
        grid_spec=pltpu.PrefetchScalarGridSpec(
            num_scalar_prefetch=1,
            grid=((hi - lo) // step,),
            in_specs=[spec(j) for j in range(step)],
            out_specs=pl.BlockSpec((step, size_b, size_b), lambda i, p: (i, 0, 0)),
        ),
        out_shape=jax.ShapeDtypeStruct((hi - lo, size_b, size_b), bf16),
        name="sorted_tiles",
    )(perm, *([master] * step))


def place_tiles(sources, parts, shapes, ids, counts, size_b):
    arrays = []
    for source in sources:
        if not any(source[0] is array for array in arrays):
            arrays.append(source[0])
    places = [next(i for i, array in enumerate(arrays) if array is source[0]) for source in sources]
    n_src, n_out = len(arrays), len(shapes)

    def kernel(ids_ref, counts_ref, *refs):
        outs, sem = refs[n_src : n_src + n_out], refs[-1]
        for m, edge, base, cols, off in parts:
            for s, (_, at, row, lo, hi) in zip(places, sources):

                def step(k, carry, s=s, m=m, base=base, cols=cols, off=off, row=row, skip=lo - at):
                    tile = ids_ref[row, k] - base
                    r = tile // cols
                    c = tile - r * cols + off
                    pltpu.make_async_copy(
                        refs[s].at[k - skip],
                        outs[m].at[
                            pl.ds(pl.multiple_of(r * size_b, size_b), size_b),
                            pl.ds(pl.multiple_of(c * size_b, size_b), size_b),
                        ],
                        sem,
                    ).start()
                    return carry

                first = jnp.maximum(counts_ref[row, edge], lo)
                last = jnp.minimum(counts_ref[row, edge + 1], hi)
                lax.fori_loop(first, last, step, 0)
        for out in outs:
            pltpu.make_async_copy(out, out, sem).wait()

    return pl.pallas_call(
        kernel,
        grid_spec=pltpu.PrefetchScalarGridSpec(
            num_scalar_prefetch=2,
            grid=(1,),
            in_specs=[pl.BlockSpec(memory_space=pl.ANY)] * n_src,
            out_specs=[pl.BlockSpec(memory_space=pltpu.VMEM)] * n_out,
            scratch_shapes=[pltpu.SemaphoreType.DMA],
        ),
        out_shape=[jax.ShapeDtypeStruct(shape, bf16) for shape in shapes],
        compiler_params=pltpu.CompilerParams(vmem_limit_bytes=60 * MIB),
        name="place_tiles",
    )(ids, counts, *arrays)


def pick_tiles(matrices, parts, ids, counts, rows, lo, hi, size_b):
    n_src, n_out = len(matrices), len(rows)

    def kernel(ids_ref, counts_ref, *refs):
        outs, sem = refs[n_src : n_src + n_out], refs[-1]
        for m, edge, base, cols, off in parts:
            for i, group in enumerate(rows):
                for j, row in enumerate(group):

                    def step(k, carry, i=i, j=j, row=row, m=m, base=base, cols=cols, off=off):
                        tile = ids_ref[row, k] - base
                        r = tile // cols
                        c = tile - r * cols + off
                        pltpu.make_async_copy(
                            refs[m].at[
                                pl.ds(pl.multiple_of(r * size_b, size_b), size_b),
                                pl.ds(pl.multiple_of(c * size_b, size_b), size_b),
                            ],
                            outs[i].at[j, k - lo],
                            sem,
                        ).start()
                        return carry

                    first = jnp.maximum(counts_ref[row, edge], lo)
                    last = jnp.minimum(counts_ref[row, edge + 1], hi)
                    lax.fori_loop(first, last, step, 0)
        for out in outs:
            pltpu.make_async_copy(out, out, sem).wait()

    return pl.pallas_call(
        kernel,
        grid_spec=pltpu.PrefetchScalarGridSpec(
            num_scalar_prefetch=2,
            grid=(1,),
            in_specs=[pl.BlockSpec(memory_space=pl.ANY)] * n_src,
            out_specs=[pl.BlockSpec(memory_space=pltpu.VMEM)] * n_out,
            scratch_shapes=[pltpu.SemaphoreType.DMA],
        ),
        out_shape=[jax.ShapeDtypeStruct((len(group), hi - lo, size_b, size_b), bf16) for group in rows],
        compiler_params=pltpu.CompilerParams(vmem_limit_bytes=60 * MIB),
        name="pick_tiles",
    )(ids, counts, *matrices)


def dot_nt(a, b):
    return lax.dot_general(a, b, (((1,), (1,)), ((), ())), preferred_element_type=f32)


def dot_tn(a, b):
    return lax.dot_general(a, b, (((0,), (0,)), ((), ())), preferred_element_type=f32)


def dot_nn(a, b):
    return lax.dot_general(a, b, (((1,), (0,)), ((), ())), preferred_element_type=f32)


def softmax_block(q_block, k_head, first, length):
    keys = k_head.shape[0]
    scores = dot_nt(q_block, k_head) * (HD**-0.5)
    rows = first + lax.broadcasted_iota(jnp.int32, scores.shape, 0)
    cols = lax.broadcasted_iota(jnp.int32, scores.shape, 1)
    scores = jnp.where((cols <= rows) & (cols < length), scores, NEG)
    probs = jnp.exp(scores - jnp.max(scores, axis=-1, keepdims=True))
    return probs / jnp.sum(probs, axis=-1, keepdims=True)


def attention(raw, scale_q, scale_k, gains, cos_t, sin_t, lengths):
    slots, width = raw.shape[0], raw.shape[1] // 3
    heads = width // HD
    block = min(256, slots)

    def kernel(len_ref, q_ref, k_ref, v_ref, sq_ref, sk_ref, gain_ref, cos_ref, sin_ref, out_ref, ql_ref, kl_ref, vl_ref):
        def turned(ref, scale, row):
            val = ref[...] * scale[...] * gain_ref[row : row + 1, :]
            return (val * cos_ref[...] + pltpu.roll(val, HD // 2, 1) * sin_ref[...]).astype(bf16)

        ql_ref[...] = turned(q_ref, sq_ref, 0)
        kl_ref[...] = turned(k_ref, sk_ref, 1)
        vl_ref[...] = v_ref[...].astype(bf16)
        for first in range(0, slots, block):
            last = first + block
            probs = softmax_block(ql_ref[first:last, :], kl_ref[:last, :], first, len_ref[0])
            out_ref[first:last, :] = dot_nn(probs.astype(bf16), vl_ref[:last, :]).astype(bf16)

    def head_spec(part):
        return pl.BlockSpec((slots, HD), lambda h, n: (0, part * heads + h))

    whole = lambda shape: pl.BlockSpec(shape, lambda h, n: (0, 0))
    out_spec = pl.BlockSpec((slots, HD), lambda h, n: (0, h))
    return pl.pallas_call(
        kernel,
        grid_spec=pltpu.PrefetchScalarGridSpec(
            num_scalar_prefetch=1,
            grid=(heads,),
            in_specs=[head_spec(0), head_spec(1), head_spec(2), whole((slots, 1)), whole((slots, 1))]
            + [pl.BlockSpec((4, HD), lambda h, n: (0, h)), whole((slots, HD)), whole((slots, HD))],
            out_specs=[out_spec] * 4,
        ),
        out_shape=[jax.ShapeDtypeStruct((slots, width), bf16)] * 4,
        compiler_params=pltpu.CompilerParams(vmem_limit_bytes=48 * MIB),
        name="attention",
    )(lengths, raw, raw, raw, scale_q, scale_k, gains, cos_t, sin_t)


def attention_back(q_low, k_low, v_low, d_attn, cos_t, sin_t, lengths):
    slots, width = q_low.shape
    heads = width // HD
    block = min(256, slots)

    def kernel(len_ref, q_ref, k_ref, v_ref, do_ref, cos_ref, sin_ref, dq_ref, dk_ref, dv_ref, dk_acc, dv_acc):
        def turned_back(val, rows):
            return val * cos_ref[rows, :] - pltpu.roll(val, HD // 2, 1) * sin_ref[rows, :]

        dk_acc[...] = jnp.zeros_like(dk_acc)
        dv_acc[...] = jnp.zeros_like(dv_acc)
        for first in range(0, slots, block):
            last = first + block
            rows, keys = slice(first, last), slice(0, last)
            probs = softmax_block(q_ref[rows, :], k_ref[keys, :], first, len_ref[0])
            d_out = do_ref[rows, :]
            d_probs = dot_nt(d_out, v_ref[keys, :])
            delta = jnp.sum(probs * d_probs, axis=-1, keepdims=True)
            d_scores = (probs * (d_probs - delta)).astype(bf16)
            dq_ref[rows, :] = turned_back(dot_nn(d_scores, k_ref[keys, :]) * (HD**-0.5), rows)
            dk_acc[keys, :] += dot_tn(d_scores, q_ref[rows, :])
            dv_acc[keys, :] += dot_tn(probs.astype(bf16), d_out)
        dk_ref[...] = turned_back(dk_acc[...] * (HD**-0.5), slice(0, slots))
        dv_ref[...] = dv_acc[...].astype(bf16)

    spec = pl.BlockSpec((slots, HD), lambda h, n: (0, h))
    whole = pl.BlockSpec((slots, HD), lambda h, n: (0, 0))
    return pl.pallas_call(
        kernel,
        grid_spec=pltpu.PrefetchScalarGridSpec(
            num_scalar_prefetch=1,
            grid=(heads,),
            in_specs=[spec] * 4 + [whole] * 2,
            out_specs=[spec] * 3,
            scratch_shapes=[pltpu.VMEM((slots, HD), f32)] * 2,
        ),
        out_shape=[
            jax.ShapeDtypeStruct((slots, width), f32),
            jax.ShapeDtypeStruct((slots, width), f32),
            jax.ShapeDtypeStruct((slots, width), bf16),
        ],
        compiler_params=pltpu.CompilerParams(vmem_limit_bytes=48 * MIB),
        name="attention_back",
    )(lengths, q_low, k_low, v_low, d_attn, cos_t, sin_t)


def renew(grads, perm, lo, held, outs):
    count, size_b = grads.shape[0], grads.shape[-1]
    n_old = 0 if outs is None else len(outs)
    batch = fit(count)
    steps = count // batch

    def kernel(perm_ref, g_ref, *refs):
        ins = [refs[a * batch : (a + 1) * batch] for a in range(5)]
        outs_ref = refs[5 * batch + n_old : 5 * batch + n_old + 4]
        held_ref, sems = refs[-2:]
        i = pl.program_id(0)
        side = i % 2

        def drain(which):
            pltpu.make_async_copy(held_ref.at[which], held_ref.at[which], sems.at[which]).wait()

        @pl.when(i >= 2)
        def _():
            drain(side)

        for j in range(batch):
            master, left_s, right_s, left_r, right_r = (ins[a][j][0] for a in range(5))
            g = g_ref[j]
            held_ref[side, 0, j] = g.astype(f32)
            held_ref[side, 1, j] = DECAY * left_s + (1.0 - DECAY) * dot_nt(g, g)
            held_ref[side, 2, j] = DECAY * right_s + (1.0 - DECAY) * dot_tn(g, g)
            left = dot_nn(left_r.astype(bf16), g).astype(bf16)
            held_ref[side, 3, j] = master - LEARN_RATE * dot_nn(left, right_r.astype(bf16))
        for j in range(batch):
            slot = perm_ref[lo + batch * i + j]
            for a in range(4):
                pltpu.make_async_copy(held_ref.at[side, a, j], outs_ref[a].at[slot], sems.at[side]).start()

        @pl.when(i == steps - 1)
        def _():
            drain(side)
            if steps > 1:
                drain(1 - side)

    def spec(j):
        return pl.BlockSpec((1, size_b, size_b), lambda i, p: (p[lo + batch * i + j], 0, 0))

    return pl.pallas_call(
        kernel,
        grid_spec=pltpu.PrefetchScalarGridSpec(
            num_scalar_prefetch=1,
            grid=(steps,),
            in_specs=[pl.BlockSpec((batch, size_b, size_b), lambda i, p: (i, 0, 0))]
            + [spec(j) for _ in range(5) for j in range(batch)]
            + [pl.BlockSpec(memory_space=pl.ANY)] * n_old,
            out_specs=[pl.BlockSpec(memory_space=pl.ANY)] * 4,
            scratch_shapes=[
                pltpu.VMEM((2, 4, batch, size_b, size_b), f32),
                pltpu.SemaphoreType.DMA((2,)),
            ],
        ),
        out_shape=[jax.ShapeDtypeStruct(held[0].shape, f32)] * 4,
        input_output_aliases={2 + 5 * batch + i: i for i in range(n_old)},
        name="renew",
    )(perm, grads, *[array for array in held for _ in range(batch)], *(outs or ()))


def rope_tables(seq_len):
    half = HD // 2
    freqs = THETA ** (-(2.0 * jnp.arange(half, dtype=f32)) / HD)
    angles = jnp.arange(seq_len, dtype=f32)[:, None] * freqs[None, :]
    cos_t, sin_t = jnp.cos(angles), jnp.sin(angles)
    return jnp.concatenate([cos_t, cos_t], 1), jnp.concatenate([-sin_t, sin_t], 1)


def core(fast, cuts, links, tables, perm, gain_full, args):
    tokens, cotangent, lengths, gains, gain_stats, gain_roots = args[:6]
    master, left_stats, right_stats, left_roots, right_roots = args[6:]
    ids, counts = tables
    size_b = master.shape[-1]
    slots, width_local = tokens.shape
    n_t = links.n_t
    width_d = width_local * n_t
    hidden_local = FF // n_t
    count = master.shape[0]

    edges, cols_w, cols_h, cols_d = tile_edges(width_local, width_d, hidden_local, size_b)
    qkv_parts = [(i, edges[i], cols_w, i * cols_w) for i in range(3)]
    o_part, gate_part, up_part, down_part = (
        (3 + i, edges[3 + i], cols, 0) for i, cols in enumerate((cols_d, cols_h, cols_h, cols_d))
    )

    edge_a, edge_b1, edge_b, count = cuts["a"], cuts["b1"], cuts["b"], cuts["end"]
    own_a = sorted_tiles(master, perm, 0, edge_a)
    later = after(perm, own_a)
    owns = [sorted_tiles(master, later, lo, hi) for lo, hi in ((edge_a, edge_b1), (edge_b1, edge_b), (edge_b, count))]
    tok_full = lax.all_gather(tokens, "tensor", axis=1, tiled=True)
    cot_full = lax.all_gather(cotangent, "tensor", axis=1, tiled=True)

    mine, theirs = [own_a], [links.swap_x(own_a)]
    for r in range(1, links.nz):
        if r == 1:
            mine.append(links.ring(own_a))
        else:
            mine.append(links.ring(after(mine[-1], theirs[r - 2], *(owns if r == 2 else ()))))
        if r > 1:
            theirs.append(links.swap_x(after(mine[r - 1], theirs[-1])))
    theirs.append(links.swap_x(after(mine[-1], theirs[-1])))
    own_b1 = links.swap_x(after(owns[0], theirs[-1]))
    own_c = links.swap_x(after(owns[2], own_b1))
    own_b2 = links.swap_x(after(owns[1], own_b1))
    sources_a = []
    for r in range(links.nz):
        sources_a.append((mine[r], 0, 2 * r, 0, edge_a))
        sources_a.append((theirs[r], 0, 2 * r + 1, 0, edge_a))

    def matrices(sources, groups, shapes):
        return place_tiles(sources, [(m,) + part for m, part in groups], shapes, ids, counts, size_b)

    def send_others(gathered, n, last):
        sent = []
        for r in range(1, links.nz):
            piece = lax.dynamic_slice_in_dim(gathered, ((links.z + r) % links.nz) * n, n, 0)
            last = links.swap_x(after(piece, last))
            sent.append(last)
        return sent

    def all_sources(lo, hi, gathered, own_x, rest_x):
        n = hi - lo
        found = [(gathered, z * n, links.n_dp + 2 * z, lo, hi) for z in range(links.nz)]
        found.append((own_x, 0, 1, lo, hi))
        return found + [(rest_x[r - 1], 0, 2 * r + 1, lo, hi) for r in range(1, links.nz)]

    n_b1, n_b2, n_c = edge_b1 - edge_a, edge_b - edge_b1, count - edge_b
    z_b1, z_b2, z_c = (
        links.gather_z(after(own, mine[-1], theirs[-2])) for own in (owns[0], owns[1], jnp.concatenate([owns[2], own_c], axis=0))
    )
    rest_b1 = send_others(z_b1, n_b1, own_b2)
    rest_b2 = send_others(z_b2, n_b2, rest_b1[-1])
    sources_b1 = sources_a + all_sources(edge_a, edge_b1, z_b1, own_b1, rest_b1)
    sources_b2 = sources_b1 + all_sources(edge_b1, edge_b, z_b2, own_b2, rest_b2)
    sources_c = sources_b2 + [
        (z_c, (2 * z + xr) * n_c, links.n_dp + 2 * z + xr, edge_b, count) for z in range(links.nz) for xr in range(2)
    ]
    if not fast:
        sources_a = sources_b1 = sources_b2 = sources_c

    gain_local = gains.astype(bf16).astype(f32)
    length = lengths[0]
    cos_t, sin_t = rope_tables(slots)
    own_rows = slots // n_t
    row0 = links.t * own_rows
    tok_rows = lax.dynamic_slice_in_dim(tok_full, row0, own_rows, 0).astype(f32)
    live = (row0 + jnp.arange(own_rows) < length).astype(f32)[:, None]
    grad_rows = lax.dynamic_slice_in_dim(cot_full, row0, own_rows, 0).astype(f32) * live

    w_qkv, w_o = matrices(
        sources_a,
        [(0, part) for part in qkv_parts] + [(1, o_part)],
        [(width_d, 3 * width_local), (width_local, width_d)],
    )
    raw = after(dot_nn(tok_full, w_qkv), own_b1)
    queries, keys_raw = raw[:, :width_local], raw[:, width_local : 2 * width_local]
    squares = lax.psum(
        jnp.stack([jnp.sum(queries * queries, axis=-1), jnp.sum(keys_raw * keys_raw, axis=-1)]), "tensor"
    )
    scale_q = lax.rsqrt(squares[0] / width_d + EPSILON)[:, None]
    scale_k = lax.rsqrt(squares[1] / width_d + EPSILON)[:, None]
    attn_low, q_low, k_low, v_low = attention(raw, scale_q, scale_k, gain_local, cos_t, sin_t, lengths)
    branch = links.reduce_rows(dot_nn(after(attn_low, own_c, own_b2), w_o).astype(bf16))
    branch = after(branch, z_b1)
    rms_a = lax.rsqrt(jnp.mean(branch * branch, axis=-1, keepdims=True) + EPSILON)
    hidden_rows = tok_rows + branch * rms_a * gain_full[2]
    hidden_low = links.gather_rows(hidden_rows.astype(bf16))
    hidden_low = after(hidden_low, rest_b1[0])

    (w_gate,) = matrices(sources_b1, [(0, gate_part)], [(width_d, hidden_local)])
    gate_act = dot_nn(hidden_low, w_gate)
    sig_gate = jax.nn.sigmoid(gate_act)
    silu_act = gate_act * sig_gate
    (w_down,) = matrices(sources_c, [(0, down_part)], [(hidden_local, width_d)])
    sources_b2 = [(after(sources_b2[0][0], w_down),) + sources_b2[0][1:]] + sources_b2[1:]
    (w_up,) = matrices(sources_b2, [(0, up_part)], [(width_d, hidden_local)])
    up_act = dot_nn(hidden_low, w_up)
    inner_low = (silu_act * up_act).astype(bf16)
    mlp_rows = links.reduce_rows(dot_nn(inner_low, w_down).astype(bf16))
    rms_m = lax.rsqrt(jnp.mean(mlp_rows * mlp_rows, axis=-1, keepdims=True) + EPSILON)
    result = hidden_rows + mlp_rows * rms_m * gain_full[3]
    scaled_m = gain_full[3] * grad_rows
    d_mlp = rms_m * scaled_m - mlp_rows * rms_m**3 * jnp.mean(scaled_m * mlp_rows, axis=-1, keepdims=True)
    d_mlp_low = links.gather_rows(d_mlp.astype(bf16))

    grads = {}
    grad_parts = [(0, down_part), (1, up_part), (2, gate_part), (3, o_part)] + [(4, p) for p in qkv_parts]
    held = (master, left_stats, right_stats, left_roots, right_roots)
    half_z = links.nz // 2
    edge_m = (edge_a + edge_b1) // 4 * 2
    abs_row = lambda z, xr: links.n_dp + 2 * z + xr
    theirs_rows = [[abs_row(z, 1) for z in range(half_z)], [abs_row(z, 1) for z in range(half_z, links.nz)]]
    mine_rows = [abs_row(z, 0) for z in range(links.nz)]

    def cut_out(lo, hi, n_mats, rows):
        parts = [(m,) + part for m, part in grad_parts if m < n_mats]
        return pick_tiles([grads[m] for m in range(n_mats)], parts, ids, counts, rows, lo, hi, size_b)

    def flat(value):
        return value.reshape((-1, size_b, size_b))

    def summed(mine, *got):
        return (flat(mine).astype(f32) + jnp.concatenate(got, axis=0).astype(f32)).astype(bf16)

    full_rows = theirs_rows + [mine_rows]
    grads[0] = dot_tn(inner_low, d_mlp_low).astype(bf16)
    if fast:
        out_a, out_b, mine_0 = cut_out(edge_b, count, 1, full_rows)
        got_0a = links.swap_x(flat(out_a))
        got_0b = links.swap_x(after(flat(out_b), got_0a))
        d_mlp_low = after(d_mlp_low, out_a)
    d_inner = dot_nt(d_mlp_low, w_down)
    d_gate = (d_inner * up_act * sig_gate * (1.0 + gate_act * (1.0 - sig_gate))).astype(bf16)
    d_up = (d_inner * silu_act).astype(bf16)
    if fast:
        d_up, d_gate = lax.optimization_barrier((d_up, d_gate, got_0a))[:2]
    grads[1] = dot_tn(hidden_low, d_up).astype(bf16)
    if fast:
        out_a, out_b, mine_1 = cut_out(edge_b1, edge_b, 2, full_rows)
        total_0 = links.reduce_z(summed(mine_0, got_0a, after(got_0b, out_a)))
        got_1a = links.swap_x(after(flat(out_a), got_0b))
        got_1b = links.swap_x(after(flat(out_b), got_1a))
        d_gate = after(d_gate, out_a, got_0b)
    grads[2] = dot_tn(hidden_low, d_gate).astype(bf16)
    d_up_in = after(d_up, grads[2])
    back_part = (dot_nt(d_gate, w_gate) + dot_nt(d_up_in, w_up)).astype(bf16)
    if fast:
        back_part = after(back_part, got_1a)
    sends = {}
    both_x = [theirs_rows[0] + theirs_rows[1], mine_rows]

    def while_reducing(both):
        grads[2] = after(grads[2], both)
        sends["2a"] = cut_out(edge_m, edge_b1, 3, both_x)
        sends["2b"] = cut_out(edge_a, edge_m, 3, both_x)
        return (sends["2b"][0],)

    def while_gathering(own):
        sum_1 = summed(mine_1, got_1a, after(got_1b, own))
        sends["outs"] = renew(after(total_0, sum_1), perm, edge_b, held, None)
        sends["1"] = links.reduce_z(sum_1)
        return (sum_1, sends["outs"][0])

    d_hidden = grad_rows + links.reduce_rows(back_part, while_reducing if fast else None)
    if fast:
        got_2a = links.swap_x(after(flat(sends["2a"][0]), got_1a))
        got_2b = links.swap_x(after(flat(sends["2b"][0]), got_2a))
    scaled_a = gain_full[2] * d_hidden
    d_branch = rms_a * scaled_a - branch * rms_a**3 * jnp.mean(scaled_a * branch, axis=-1, keepdims=True)
    d_branch_low = links.gather_rows(d_branch.astype(bf16), while_gathering if fast else None)
    d_attn = dot_nt(d_branch_low, w_o).astype(bf16)
    if fast:
        sum_2a = summed(sends["2a"][1], after(got_2a, d_attn))
        total_2a = links.reduce_z(sum_2a)
        d_attn = after(d_attn, sum_2a)
        total_1, outs = sends["1"], sends["outs"]
    d_qn, d_kn, d_values = attention_back(q_low, k_low, v_low, d_attn, cos_t, sin_t, lengths)
    scaled_q = gain_local[0] * d_qn
    scaled_k = gain_local[1] * d_kn
    gain_m_all = jnp.sum(grad_rows * mlp_rows * rms_m, axis=0)
    gain_a_all = jnp.sum(d_hidden * branch * rms_a, axis=0)
    sums = lax.psum(
        jnp.concatenate(
            [
                jnp.sum(scaled_q * queries, axis=-1),
                jnp.sum(scaled_k * keys_raw, axis=-1),
                gain_a_all,
                gain_m_all,
            ]
        ),
        "tensor",
    )
    stat_q, stat_k = sums[:slots], sums[slots : 2 * slots]
    gain_a_all, gain_m_all = sums[2 * slots : 2 * slots + width_d], sums[2 * slots + width_d :]
    d_queries = scale_q * scaled_q - queries * scale_q**3 * (stat_q / width_d)[:, None]
    d_keys = scale_k * scaled_k - keys_raw * scale_k**3 * (stat_k / width_d)[:, None]
    d_qkv = jnp.concatenate([d_queries.astype(bf16), d_keys.astype(bf16), d_values], axis=1)
    grads[4] = dot_tn(tok_full, d_qkv).astype(bf16)
    grads[3] = dot_tn(attn_low, d_branch_low).astype(bf16)
    if not fast:
        totals = []
        for lo, hi in ((edge_b, count), (edge_b1, edge_b), (edge_m, edge_b1), (edge_a, edge_m)):
            out_a, out_b, mine_n = cut_out(lo, hi, 5, full_rows)
            got_2a, got_2b = links.swap_x(flat(out_a)), links.swap_x(flat(out_b))
            totals.append(links.reduce_z(summed(mine_n, got_2a, got_2b)))
        total_0, total_1, total_2a, total_2b = totals
        outs = renew(total_0, perm, edge_b, held, None)

    mid = edge_a // 4 * 2
    turns = list(range(1, links.nz)) + [0]
    first_cut = cut_out(0, edge_a, 5, [[2 * turns[0] + 1], [2 * turns[0]]])
    grads[4] = after(grads[4], first_cut[0])
    rest = cut_out(0, edge_a, 5, [[2 * r + 1] for r in turns[1:]] + [[2 * r for r in turns[1:]]])
    to_send = [first_cut[0][0]] + [rest[k][0] for k in range(links.nz - 1)]
    to_keep = [first_cut[1][0]] + [rest[-1][k] for k in range(links.nz - 1)]
    pins = (rest[0],)
    late = [(edge_b1, total_1), (edge_m, total_2a), (edge_a, total_2b)] if not fast else []
    if fast:
        sum_2b = summed(sends["2b"][1], after(got_2b, rest[0]))
        total_2b = links.reduce_z(sum_2b)
        pins = (rest[0], sum_2b)
        late = [(edge_b1, total_1), (edge_m, total_2a), (edge_a, total_2b)]

    def joined(kept, got, ring):
        total = kept.astype(f32) + got.astype(f32)
        if ring is not None:
            total = total + ring.astype(f32)
        return total.astype(bf16)

    x_done = [got_2a, got_2b]
    ring = None
    for event in range(links.nz - 2):
        got = links.swap_x(after(to_send[event], x_done[-2]))
        x_done.append(got)
        total = joined(to_keep[event], after(got, *pins), ring)
        ring = links.ring(total)
        if event == 0:
            input_part = dot_nt(after(d_qkv, total), w_qkv).astype(bf16)
            pins = (input_part,)
        elif late:
            lo, ready = late.pop(0)
            outs = renew(after(ready, total), perm, lo, held, outs)
            pins = (outs[0],)
    halves = ((0, mid), (mid, edge_a))
    last_rings = []
    for lo, hi in halves:
        got = links.swap_x(after(to_send[-2][lo:hi], x_done[-2]))
        x_done.append(got)
        total = joined(to_keep[-2][lo:hi], after(got, *pins), ring[lo:hi])
        last_rings.append(links.ring(total))
        pins = ()
        if late:
            at, ready = late.pop(0)
            outs = renew(after(ready, total), perm, at, held, outs)
            pins = (outs[0],)
    gain_start = total
    for (lo, hi), ring in zip(halves, last_rings):
        got = links.swap_x(after(to_send[-1][lo:hi], x_done[-2]))
        x_done.append(got)
        total = joined(to_keep[-1][lo:hi], after(got, *pins), ring)
        pins = ()
        outs = renew(total, perm, lo, held, outs)

    input_rows = links.reduce_rows(input_part)
    token_grads = links.rows_to_cols((input_rows + d_hidden).astype(bf16))
    block_out = links.rows_to_cols(after(result, x_done[3]).astype(bf16))

    gain_terms = jnp.stack(
        [
            jnp.sum(d_qn * queries * scale_q, axis=0),
            jnp.sum(d_kn * keys_raw * scale_k, axis=0),
            lax.dynamic_slice_in_dim(gain_a_all, links.t * width_local, width_local, 0),
            lax.dynamic_slice_in_dim(gain_m_all, links.t * width_local, width_local, 0),
        ]
    )
    gain_terms = after(gain_terms, gain_start)
    gain_part = gain_terms + links.swap_x(gain_terms)
    gain_grads = gain_part
    for r in range(1, links.nz):
        gain_part = links.ring(gain_part)
        gain_grads = gain_grads + gain_part
    gain_stats_new = DECAY * gain_stats + (1.0 - DECAY) * gain_grads * gain_grads
    gains_new = gains - GAIN_RATE * gain_grads * gain_roots

    block_grads, left_new, right_new, master_new = (out[None] for out in outs)
    return (
        block_out,
        token_grads,
        block_grads,
        left_new,
        right_new,
        master_new,
        gain_grads,
        gain_stats_new,
        gains_new,
    )


def tile_edges(width_local, width_d, hidden_local, size_b):
    cols_w, cols_h, cols_d = width_local // size_b, hidden_local // size_b, width_d // size_b
    sizes = [cols_d * cols_w] * 4 + [cols_d * cols_h] * 3
    return [sum(sizes[:i]) for i in range(8)], cols_w, cols_h, cols_d


def cut_points(count):
    def at(part):
        return count * part // 128 // 2 * 2

    a, b1, b = at(48), at(84), at(112)
    return {"a": a, "b1": b1, "b": b, "end": count}


def body(
    tokens,
    cotangent,
    lengths,
    gains,
    gain_stats,
    gain_roots,
    master,
    block_order,
    left_stats,
    right_stats,
    left_roots,
    right_roots,
):
    links = Links()
    count, size_b = master.shape[1], master.shape[-1]
    cuts = cut_points(count)
    order = block_order[0].reshape(links.n_dp, count)
    rank = jnp.sum(order[:, None, :] < order[:, :, None], axis=2, dtype=jnp.int32)
    hit = rank[:, None, :] == jnp.arange(count)[None, :, None]
    sorted_ids = jnp.sum(jnp.where(hit, order[:, None, :], 0), axis=2, dtype=jnp.int32)
    rank_own = lax.dynamic_index_in_dim(rank, links.d, 0, False)
    perm = jnp.sum(
        jnp.where(rank_own[None, :] == jnp.arange(count)[:, None], jnp.arange(count)[None, :], 0),
        axis=1,
        dtype=jnp.int32,
    )
    width_local = tokens.shape[1]
    edges = tile_edges(width_local, width_local * links.n_t, FF // links.n_t, size_b)[0]
    counts = jnp.sum(order[:, None, :] < jnp.asarray(edges, jnp.int32)[None, :, None], axis=2, dtype=jnp.int32)
    fits = jnp.all((counts[:, 4] <= cuts["a"]) & (counts[:, 5] <= cuts["b1"]) & (counts[:, 6] <= cuts["b"]))

    table = jnp.concatenate([sorted_ids, counts], axis=1).reshape(links.nz, 2, count + 8)
    table = jnp.where(links.x == 0, table, table[:, ::-1])
    twice = jnp.concatenate([table, table], axis=0)
    ring = lax.dynamic_slice_in_dim(twice, links.z, links.nz, 0)
    table = jnp.concatenate([ring, table], axis=0).reshape(2 * links.n_dp, count + 8)
    tables = (table[:, :count], table[:, count:])
    flag = jnp.broadcast_to(jnp.where(fits, 1.0, 0.0), (1, tokens.shape[1]))
    shared = lax.all_gather(
        jnp.concatenate([gains, flag], axis=0).astype(bf16), "tensor", axis=1, tiled=True
    ).astype(f32)
    gain_full, all_fit = shared[:4], jnp.min(shared[4]) > 0.5
    args = (tokens, cotangent, lengths, gains, gain_stats, gain_roots)
    args = args + (master[0], left_stats[0], right_stats[0], left_roots[0], right_roots[0])

    def run(fast):
        return lambda *rest: core(fast, cuts, links, tables, perm, gain_full, rest)

    if MODE == "fast":
        return run(True)(*args)
    return lax.cond(all_fit, run(True), run(False), *args)


MODE = "cond"


def solution(mesh):
    placed = (
        P("dp", "tensor"),
        P("dp", "tensor"),
        P("dp"),
        P(None, "tensor"),
        P(None, "tensor"),
        P(None, "tensor"),
        P("tensor", "dp", None, None),
        P("tensor", None),
        P("tensor", "dp", None, None),
        P("tensor", "dp", None, None),
        P("tensor", "dp", None, None),
        P("tensor", "dp", None, None),
    )
    return jax.shard_map(
        body,
        mesh=mesh,
        in_specs=placed,
        out_specs=(
            P("dp", "tensor"),
            P("dp", "tensor"),
            P("tensor", "dp", None, None),
            P("tensor", "dp", None, None),
            P("tensor", "dp", None, None),
            P("tensor", "dp", None, None),
            P(None, "tensor"),
            P(None, "tensor"),
            P(None, "tensor"),
        ),
        check_vma=False,
    )
```

time: 2180 us -> 1080 us (0.50)
  waiting for transfers between devices: 1330 us -> 462 us
  local copies, waits for them, and re-layouts: 427 us -> 47.7 us
  Pallas kernels: 0 us -> 199 us
  matrix products: 260 us -> 163 us
  starting transfers between devices: 0.73 us -> 72.5 us
    all_gather x3 -> x5, waiting for transfers between devices: 662 us -> 0.05 us  [the longest x3 0.02 us: gather_z(): lax.all_gather(value, 'dp', axis=0, tiled=True, axis_index_groups=self.z_...]
    reduce_scatter x2 -> x4, waiting for transfers between devices: 510 us -> 0.03 us  [reduce_z(): lax.psum_scatter(value, 'dp', scatter_dimension=0, tiled=True, axis_index...]
    ppermute x0 -> x59, waiting for transfers between devices: none -> 461 us  [the longest x26 267 us: swap_x(): return lax.ppermute(value, 'dp', [(i, i ^ 1) for i in range(self.n_dp)])]
    pallas_call x0 -> x25, Pallas kernels: none -> 199 us  [the longest x6 58.8 us: renew(): pl.pallas_call(kernel, grid_spec=pltpu.PrefetchScalarGridSpec(num_scalar_...]
    psum x3 -> x0, waiting for transfers between devices: 161 us -> none  [the longest x1 85.1 us: body(): lax.psum(mlp_part.astype(jnp.bfloat16), 'tensor').astype(jnp.float32)]
    scatter x1 -> x0, local copies, waits for them, and re-layouts: 149 us -> none  [body(): local_stack = jnp.zeros_like(gathered).at[slot_order].set(gathered)]
    dot_general x30 -> x15, matrix products: 247 us -> 163 us  [the longest x5 58.8 us: dot_nt(): lax.dot_general(a, b, (((1,), (1,)), ((), ())), preferred_element_type=f32)]
    unnamed x194 -> x0, local copies, waits for them, and re-layouts: 80.8 us -> none
  transfers between devices with their start and end apart: 8 -> 68, of which waited for: 6 -> 32; matrix products, arithmetic and copies ran while one was open for 22% -> 23% of each run, Pallas kernels for 0% -> 16%
where the time goes in v1:
time: 1080 us; the launch traced here: 1070 us
  waiting for transfers between devices  462 us (43%)
  Pallas kernels  199 us (18%)
  matrix products  163 us (15%)
  other arithmetic  81.6 us (8%)
  starting transfers between devices  72.5 us (7%)
  local copies, waits for them, and re-layouts  47.7 us (4%)
  blocking collectives  23.8 us (2%)
  between operations  15.7 us (1%)
    ppermute x26, waiting for transfers between devices, swap_x(): return lax.ppermute(value, 'dp', [(i, i ^ 1) for i in range(self.n_dp)])  267 us
    ppermute x10, waiting for transfers between devices, ring(): return lax.ppermute(value, 'dp', pairs)  118 us
    ppermute x7, waiting for transfers between devices, shift_y(): return lax.ppermute(value, 'tensor', pairs)  61.2 us
    pallas_call x6, Pallas kernels, renew(): pl.pallas_call(kernel, grid_spec=pltpu.PrefetchScalarGridSpec(num_scalar_...  58.8 us
    dot_general x5, matrix products, dot_nt(): lax.dot_general(a, b, (((1,), (1,)), ((), ())), preferred_element_type=f32)  58.8 us
    dot_general x5, matrix products, dot_tn(): lax.dot_general(a, b, (((0,), (0,)), ((), ())), preferred_element_type=f32)  52.4 us
    dot_general x5, matrix products, dot_nn(): lax.dot_general(a, b, (((1,), (0,)), ((), ())), preferred_element_type=f32)  52.3 us
    pallas_call x6, Pallas kernels, pick_tiles(): pl.pallas_call(kernel, grid_spec=pltpu.PrefetchScalarGridSpec(num_scalar_...  42.6 us
  transfers between devices with their start and end apart: 68, of which 32 were waited for; matrix products, arithmetic and copies ran while one was open for 23% of the time, Pallas kernels for 16%

profile of v1, /device:TPU:0, one launch (start us, length us, event | category | flops | bytes accessed | tf_op | source)
XLA Modules:
  0.0 1074.3 jit_solution(5733818214113377511)
XLA Ops:
  20.2 1047.0 %conditional.1 = (bf16[1024,512]{1,0:T(8,128)(2,1)}, bf16[1024,512]{1,0:T(8,128)(2,1)}, f32[1,128,128,128]{3,2,1,0:T(8,128)}, f32[1,128,128,128]{3,2,1,0:T(8,128...) conditional(s32[]{:T(128)} %convert_element_type.615, ...), branch_computations={%region_6.25_spmd, %region_25.44_spmd} | conditional | flops 103285186560 | bytes 1469786368 | solution.py:804
  52.9 18.1 %collective-permute-done.62.refs_2_ = bf16[48,128,128]{2,1,0:T(8,128)(2,1)S(1)} collective-permute-done((bf16[48,128,128]{2,1,0:T(8,128)(2,1)}, bf16[48,128,128]{2,1,0:T(8,128)(2,1)S(1)}, u32[]{:S(2)}, u32[]{:S(2)}) %collective-permute-start.62) | collective-permute-done | bytes 1572896 | tf_op jit(solution)/shard_map/cond/branch_1_fun/ppermute | solution.py:41
  76.8 31.9 %collective-permute-done.63.refs_3_ = bf16[48,128,128]{2,1,0:T(8,128)(2,1)S(1)} collective-permute-done((bf16[48,128,128]{2,1,0:T(8,128)(2,1)S(1)}, bf16[48,128,128]{2,1,0:T(8,128)(2,1)S(1)}, u32[]{:S(2)}, u32[]{:S(2)}) %collective-permute-start.63) | collective-permute-done | bytes 1572896 | tf_op jit(solution)/shard_map/cond/branch_1_fun/ppermute | solution.py:52
  114.7 31.6 %collective-permute-done.66.refs_6_ = bf16[48,128,128]{2,1,0:T(8,128)(2,1)S(1)} collective-permute-done((bf16[48,128,128]{2,1,0:T(8,128)(2,1)S(1)}, bf16[48,128,128]{2,1,0:T(8,128)(2,1)S(1)}, u32[]{:S(2)}, u32[]{:S(2)}) %collective-permute-start.66) | collective-permute-done | bytes 1572896 | tf_op jit(solution)/shard_map/cond/branch_1_fun/ppermute | solution.py:41
  149.3 34.0 %collective-permute-done.67.refs_7_ = bf16[48,128,128]{2,1,0:T(8,128)(2,1)} collective-permute-done((bf16[48,128,128]{2,1,0:T(8,128)(2,1)}, bf16[48,128,128]{2,1,0:T(8,128)(2,1)}, u32[]{:S(2)}, u32[]{:S(2)}) %collective-permute-start.67) | collective-permute-done | bytes 1572896 | tf_op jit(solution)/shard_map/cond/branch_1_fun/ppermute | solution.py:52
  195.8 13.8 %collective-permute-done.68.refs_9_ = bf16[36,128,128]{2,1,0:T(8,128)(2,1)} collective-permute-done((bf16[36,128,128]{2,1,0:T(8,128)(2,1)}, bf16[36,128,128]{2,1,0:T(8,128)(2,1)}, u32[]{:S(2)}, u32[]{:S(2)}) %collective-permute-start.68) | collective-permute-done | bytes 1179680 | tf_op jit(solution)/shard_map/cond/branch_1_fun/ppermute | solution.py:52
  230.1 16.3 %attention.3 = (bf16[1024,512]{1,0:T(8,128)(2,1)S(1)}, bf16[1024,512]{1,0:T(8,128)(2,1)S(1)}, bf16[1024,512]{1,0:T(8,128)(2,1)S(1)}, bf16[1024,512]{1,0:T(8,128)(2,1)}) custom-call(s32[1]{0:T(128)} %get-tuple-element.189.len_ref, f32[1024,1536]{1,0:T(8,128)} %copy-done.30, f32[1024,1536]{1,0:T(8,128)} %copy-done.30, f32[1024,1536]{1,0:T(8,128)} %copy-done.30, ...), custom_call_target="tpu_custom_call" | custom-call | tf_op jit(solution)/shard_map/cond/branch_1_fun/attention/pallas_call | solution.py:298
  264.0 23.4 %collective-permute-done.76.refs_10_ = bf16[36,128,128]{2,1,0:T(8,128)(2,1)} collective-permute-done((bf16[36,128,128]{2,1,0:T(8,128)(2,1)S(1)}, bf16[36,128,128]{2,1,0:T(8,128)(2,1)}, u32[]{:S(2)}, u32[]{:S(2)}) %collective-permute-start.76) | collective-permute-done | bytes 1179680 | tf_op jit(solution)/shard_map/cond/branch_1_fun/ppermute | solution.py:52
  290.6 24.7 %collective-permute-done.77.refs_11_ = bf16[36,128,128]{2,1,0:T(8,128)(2,1)S(1)} collective-permute-done((bf16[36,128,128]{2,1,0:T(8,128)(2,1)}, bf16[36,128,128]{2,1,0:T(8,128)(2,1)S(1)}, u32[]{:S(2)}, u32[]{:S(2)}) %collective-permute-start.77) | collective-permute-done | bytes 1179680 | tf_op jit(solution)/shard_map/cond/branch_1_fun/ppermute | solution.py:52
  324.8 17.6 %collective-permute-done.78.refs_12_ = bf16[36,128,128]{2,1,0:T(8,128)(2,1)} collective-permute-done((bf16[36,128,128]{2,1,0:T(8,128)(2,1)}, bf16[36,128,128]{2,1,0:T(8,128)(2,1)}, u32[]{:S(2)}, u32[]{:S(2)}) %collective-permute-start.78) | collective-permute-done | bytes 1179680 | tf_op jit(solution)/shard_map/cond/branch_1_fun/ppermute | solution.py:52
  344.4 18.3 %collective-permute-done.79.refs_15_ = bf16[28,128,128]{2,1,0:T(8,128)(2,1)} collective-permute-done((bf16[28,128,128]{2,1,0:T(8,128)(2,1)S(1)}, bf16[28,128,128]{2,1,0:T(8,128)(2,1)}, u32[]{:S(2)}, u32[]{:S(2)}) %collective-permute-start.79) | collective-permute-done | bytes 917536 | tf_op jit(solution)/shard_map/cond/branch_1_fun/ppermute | solution.py:52
  384.9 14.5 %fusion.81 = f32[1024,2048]{1,0:T(8,128)} fusion(bf16[1024,2048]{1,0:T(8,128)(2,1)} %copy-done, bf16[2048,2048]{1,0:T(8,128)(2,1)} %place_tiles.13), kind=kOutput, calls=%fused_computation.319 | convolution fusion | flops 8589934592 | bytes 20971520 | tf_op jit(solution)/shard_map/cond/branch_1_fun/dot_general | solution.py:262
  422.3 16.4 %multiply_convert_fusion.5 = (bf16[1024,2048]{1,0:T(8,128)(2,1)S(1)}, f32[1024,2048]{1,0:T(8,128)}) fusion(f32[1024,2048]{1,0:T(8,128)} %fusion.81, bf16[1024,2048]{1,0:T(8,128)(2,1)} %copy-done, bf16[2048,2048]{1,0:T(8,128)(2,1)} %place_tiles.15), kind=kOutput, calls=%fused_computation.148 | convolution fusion | flops 8602517504 | bytes 33554432 | tf_op jit(solution)/shard_map/cond/branch_1_fun/dot_general | solution.py:262
  455.5 23.0 %collective-permute-done.83 = bf16[256,2048]{1,0:T(8,128)(2,1)S(1)} collective-permute-done((bf16[256,2048]{1,0:T(8,128)(2,1)S(1)}, bf16[256,2048]{1,0:T(8,128)(2,1)S(1)}, u32[]{:S(2)}, u32[]{:S(2)}) %collective-permute-start.83) | collective-permute-done | bytes 1048608 | tf_op jit(solution)/shard_map/cond/branch_1_fun/ppermute | solution.py:59
  486.6 22.8 %collective-permute-done.85.refs_2_ = bf16[256,2048]{1,0:T(8,128)(2,1)S(1)} collective-permute-done((bf16[256,2048]{1,0:T(8,128)(2,1)S(1)}, bf16[256,2048]{1,0:T(8,128)(2,1)S(1)}, u32[]{:S(2)}, u32[]{:S(2)}) %collective-permute-start.85) | collective-permute-done | bytes 1048608 | tf_op jit(solution)/shard_map/cond/branch_1_fun/ppermute | solution.py:59
  534.0 20.5 %multiply_convert_fusion.3 = (bf16[1024,2048]{1,0:T(8,128)(2,1)}, bf16[1024,2048]{1,0:T(8,128)(2,1)}) fusion(f32[1024,2048]{1,0:T(8,128)} %fusion.81, f32[1024,2048]{1,0:T(8,128)} %get-tuple-element.450, bf16[1024,2048]{1,0:T(8,128)(2,1)} %copy-done.7, bf16[2048,2048]{1,0:T(8,128)(2,1)} %place_tiles.14), kind=kOutput, calls=%fused_computation.146 | convolution fusion | flops 8617197568 | bytes 37748736 | tf_op jit(solution)/shard_map/cond/branch_1_fun/dot_general | solution.py:254
  559.5 14.0 %convolution_convert_fusion.11.refs_1_ = bf16[2048,2048]{1,0:T(8,128)(2,1)} fusion(bf16[1024,2048]{1,0:T(8,128)(2,1)} %copy-done, bf16[1024,2048]{1,0:T(8,128)(2,1)} %get-tuple-element.233), kind=kOutput, calls=%fused_computation.153 | convolution fusion | flops 8594128896 | bytes 16777216 | tf_op jit(solution)/shard_map/cond/branch_1_fun/dot_general | solution.py:258
  583.9 14.4 %convolution_convert_fusion.10.refs_2_ = bf16[2048,2048]{1,0:T(8,128)(2,1)} fusion(bf16[1024,2048]{1,0:T(8,128)(2,1)} %copy-done, bf16[1024,2048]{1,0:T(8,128)(2,1)} %get-tuple-element.232), kind=kOutput, calls=%fused_computation.152 | convolution fusion | flops 8594128896 | bytes 16777216 | tf_op jit(solution)/shard_map/cond/branch_1_fun/dot_general | solution.py:258
  702.1 30.1 %collective-permute-done.96 = bf16[72,128,128]{2,1,0:T(8,128)(2,1)} collective-permute-done((bf16[72,128,128]{2,1,0:T(8,128)(2,1)}, bf16[72,128,128]{2,1,0:T(8,128)(2,1)}, u32[]{:S(2)}, u32[]{:S(2)}) %collective-permute-start.96) | collective-permute-done | bytes 2359328 | tf_op jit(solution)/shard_map/cond/branch_1_fun/ppermute | solution.py:52
  744.6 17.4 %attention_back.3 = (f32[1024,512]{1,0:T(8,128)}, f32[1024,512]{1,0:T(8,128)}, bf16[1024,512]{1,0:T(8,128)(2,1)S(1)}) custom-call(s32[1]{0:T(128)} %get-tuple-element.189.len_ref, bf16[1024,512]{1,0:T(8,128)(2,1)S(1)} %copy-done.9, bf16[1024,512]{1,0:T(8,128)(2,1)S(1)} %copy-done.11, bf16[1024,512]{1,0:T(8,128)(2,1)S(1)} %copy-done.12, ...), custom_call_target="tpu_custom_call" | custom-call | tf_op jit(solution)/shard_map/cond/branch_1_fun/attention_back/pallas_call | solution.py:340
  818.5 17.2 %collective-permute-done.102 = bf16[48,128,128]{2,1,0:T(8,128)(2,1)} collective-permute-done((bf16[48,128,128]{2,1,0:T(8,128)(2,1)}, bf16[48,128,128]{2,1,0:T(8,128)(2,1)}, u32[]{:S(2)}, u32[]{:S(2)}) %collective-permute-start.102) | collective-permute-done | bytes 1572896 | tf_op jit(solution)/shard_map/cond/branch_1_fun/ppermute | solution.py:52
  859.7 29.1 %collective-permute-done.98 = bf16[48,128,128]{2,1,0:T(8,128)(2,1)} collective-permute-done((bf16[48,128,128]{2,1,0:T(8,128)(2,1)}, bf16[48,128,128]{2,1,0:T(8,128)(2,1)}, u32[]{:S(2)}, u32[]{:S(2)}) %collective-permute-start.98) | collective-permute-done | bytes 1572896 | tf_op jit(solution)/shard_map/cond/branch_1_fun/ppermute | solution.py:52
  893.6 32.3 %collective-permute-done.111 = bf16[48,128,128]{2,1,0:T(8,128)(2,1)} collective-permute-done((bf16[48,128,128]{2,1,0:T(8,128)(2,1)}, bf16[48,128,128]{2,1,0:T(8,128)(2,1)}, u32[]{:S(2)}, u32[]{:S(2)}) %collective-permute-start.111) | collective-permute-done | bytes 1572896 | tf_op jit(solution)/shard_map/cond/branch_1_fun/ppermute | solution.py:41
  988.7 32.6 %collective-permute-done.117 = f32[4,512]{1,0:T(4,128)S(1)} collective-permute-done((f32[4,512]{1,0:T(4,128)S(1)}, f32[4,512]{1,0:T(4,128)S(1)}, u32[]{:S(2)}, u32[]{:S(2)}) %collective-permute-start.117) | collective-permute-done | bytes 8224 | tf_op jit(solution)/shard_map/cond/branch_1_fun/ppermute | solution.py:41
  (454 shorter events, 536.4 us)
Async XLA Ops:
  26.4 183.8 %all-gather.21.cloned.1.call-start = ((), (), s32[]{:S(2)}) async-start(), calls=%async_computation.17 | async-start | bytes 5242880 | tf_op jit(solution)/shard_map/cond/branch_1_fun/all_gather | solution.py:450
  27.1 227.9 %all-gather.23.cloned.1.call-start = ((), (), s32[]{:S(2)}) async-start(), calls=%async_computation.18 | async-start | bytes 5898240 | tf_op jit(solution)/shard_map/cond/branch_1_fun/all_gather | solution.py:44
  148.6 173.0 %all-gather.25.cloned.1.call-start = ((), (), s32[]{:S(2)}) async-start(), calls=%async_computation.19 | async-start | bytes 4587520 | tf_op jit(solution)/shard_map/cond/branch_1_fun/all_gather | solution.py:44
  183.8 215.6 %all-gather.27.cloned.1.call-start = ((), (), s32[]{:S(2)}) async-start(), calls=%async_computation.20 | async-start | bytes 5242880 | tf_op jit(solution)/shard_map/cond/branch_1_fun/all_gather | solution.py:44
  254.8 225.0 %all-gather.29.cloned.1.call-start = ((), (), s32[]{:S(2)}) async-start(), calls=%async_computation.21 | async-start | bytes 5242880 | tf_op jit(solution)/shard_map/cond/branch_1_fun/all_gather | solution.py:451
  364.2 330.1 %reduce-scatter.17.cloned.1.call-start = ((), (), s32[]{:S(2)}) async-start(), calls=%async_computation.22 | async-start | bytes 2621440 | tf_op jit(solution)/shard_map/cond/branch_1_fun/reduce_scatter | solution.py:47
  582.4 42.1 %collective-permute-start.89 = (bf16[56,128,128]{2,1,0:T(8,128)(2,1)}, bf16[56,128,128]{2,1,0:T(8,128)(2,1)}, u32[]{:S(2)}, u32[]{:S(2)}) collective-permute-start(bf16[56,128,128]{2,1,0:T(8,128)(2,1)} %bitcast.446), channel_id=1, source_target_pairs={{0,4},{4,0},{8,12},{12,8},{16,20},{20,16},{24,28},{28,24},{1,5},{5... | collective-permute-start | bytes 5505032 | tf_op jit(solution)/shard_map/cond/branch_1_fun/ppermute | solution.py:52
  631.8 320.1 %reduce-scatter.21.cloned.1.call-start = ((), (), s32[]{:S(2)}) async-start(), calls=%async_computation.24 | async-start | bytes 4587520 | tf_op jit(solution)/shard_map/cond/branch_1_fun/reduce_scatter | solution.py:47
  639.5 43.2 %collective-permute-start.95 = (bf16[56,128,128]{2,1,0:T(8,128)(2,1)}, bf16[56,128,128]{2,1,0:T(8,128)(2,1)}, u32[]{:S(2)}, u32[]{:S(2)}) collective-permute-start(bf16[56,128,128]{2,1,0:T(8,128)(2,1)} %bitcast.100), channel_id=1, source_target_pairs={{0,4},{4,0},{8,12},{12,8},{16,20},{20,16},{24,28},{28,24},{1,5},{5... | collective-permute-start | bytes 5505032 | tf_op jit(solution)/shard_map/cond/branch_1_fun/ppermute | solution.py:52
  653.4 78.8 %collective-permute-start.96 = (bf16[72,128,128]{2,1,0:T(8,128)(2,1)}, bf16[72,128,128]{2,1,0:T(8,128)(2,1)}, u32[]{:S(2)}, u32[]{:S(2)}) collective-permute-start(bf16[72,128,128]{2,1,0:T(8,128)(2,1)} %bitcast.445), channel_id=1, source_target_pairs={{0,4},{4,0},{8,12},{12,8},{16,20},{20,16},{24,28},{28,24},{1,5},{5... | collective-permute-start | bytes 7077896 | tf_op jit(solution)/shard_map/cond/branch_1_fun/ppermute | solution.py:52
  687.2 280.3 %reduce-scatter.19.cloned.1.call-start = ((), (), s32[]{:S(2)}) async-start(), calls=%async_computation.23 | async-start | bytes 2949120 | tf_op jit(solution)/shard_map/cond/branch_1_fun/reduce_scatter | solution.py:47
  693.7 39.5 %collective-permute-start.94 = (bf16[256,2048]{1,0:T(8,128)(2,1)S(1)}, bf16[256,2048]{1,0:T(8,128)(2,1)}, u32[]{:S(2)}, u32[]{:S(2)}) collective-permute-start(bf16[256,2048]{1,0:T(8,128)(2,1)S(1)} %collective-permute-done.93.refs_2_), channel_id=1, source_target_pairs={{0,1},{1,0},{2,3},{3,2},{4,5},{5,4},{6,7},{7,6},{8,9},{9,8},{10,11... | collective-permute-start | bytes 3145736 | tf_op jit(solution)/shard_map/cond/branch_1_fun/ppermute | solution.py:55
  693.7 39.5 %collective-permute-start.92 = (bf16[256,2048]{1,0:T(8,128)(2,1)S(1)}, bf16[256,2048]{1,0:T(8,128)(2,1)}, u32[]{:S(2)}, u32[]{:S(2)}) collective-permute-start(bf16[256,2048]{1,0:T(8,128)(2,1)S(1)} %subtract_convert_fusion.6.refs_0_), channel_id=1, source_target_pairs={{0,1},{1,0},{2,3},{3,2},{4,5},{5,4},{6,7},{7,6},{8,9},{9,8},{10,11... | collective-permute-start | bytes 3145736 | tf_op jit(solution)/shard_map/cond/branch_1_fun/ppermute | solution.py:55
  732.2 80.8 %collective-permute-start.97 = (bf16[72,128,128]{2,1,0:T(8,128)(2,1)}, bf16[72,128,128]{2,1,0:T(8,128)(2,1)}, u32[]{:S(2)}, u32[]{:S(2)}) collective-permute-start(bf16[72,128,128]{2,1,0:T(8,128)(2,1)} %bitcast.444), channel_id=1, source_target_pairs={{0,4},{4,0},{8,12},{12,8},{16,20},{20,16},{24,28},{28,24},{1,5},{5... | collective-permute-start | bytes 7077896 | tf_op jit(solution)/shard_map/cond/branch_1_fun/ppermute | solution.py:52
  800.7 232.8 %reduce-scatter.23.cloned.1.call-start = ((), (), s32[]{:S(2)}) async-start(), calls=%async_computation.25 | async-start | bytes 2949120 | tf_op jit(solution)/shard_map/cond/branch_1_fun/reduce_scatter | solution.py:47
  852.4 73.4 %collective-permute-start.111 = (bf16[48,128,128]{2,1,0:T(8,128)(2,1)}, bf16[48,128,128]{2,1,0:T(8,128)(2,1)}, u32[]{:S(2)}, u32[]{:S(2)}) collective-permute-start(bf16[48,128,128]{2,1,0:T(8,128)(2,1)} %fusion.46), channel_id=1, source_target_pairs={{0,24},{4,28},{8,0},{12,4},{16,8},{20,12},{24,16},{28,20},{1,25},{... | collective-permute-start | bytes 4718600 | tf_op jit(solution)/shard_map/cond/branch_1_fun/ppermute | solution.py:41
  858.6 76.6 %collective-permute-start.110 = (bf16[24,128,128]{2,1,0:T(8,128)(2,1)S(1)}, bf16[24,128,128]{2,1,0:T(8,128)(2,1)S(1)}, u32[]{:S(2)}, u32[]{:S(2)}) collective-permute-start(bf16[24,128,128]{2,1,0:T(8,128)(2,1)S(1)} %get-tuple-element.280), channel_id=1, source_target_pairs={{0,4},{4,0},{8,12},{12,8},{16,20},{20,16},{24,28},{28,24},{1,5},{5... | collective-permute-start | bytes 2359304 | tf_op jit(solution)/shard_map/cond/branch_1_fun/ppermute | solution.py:52
  888.9 55.5 %collective-permute-start.108 = (bf16[24,128,128]{2,1,0:T(8,128)(2,1)S(1)}, bf16[24,128,128]{2,1,0:T(8,128)(2,1)S(1)}, u32[]{:S(2)}, u32[]{:S(2)}) collective-permute-start(bf16[24,128,128]{2,1,0:T(8,128)(2,1)S(1)} %get-tuple-element.278), channel_id=1, source_target_pairs={{0,4},{4,0},{8,12},{12,8},{16,20},{20,16},{24,28},{28,24},{1,5},{5... | collective-permute-start | bytes 2359304 | tf_op jit(solution)/shard_map/cond/branch_1_fun/ppermute | solution.py:52
  892.4 53.0 %collective-permute-start.104 = (bf16[256,2048]{1,0:T(8,128)(2,1)S(1)}, bf16[256,2048]{1,0:T(8,128)(2,1)S(1)}, u32[]{:S(2)}, u32[]{:S(2)}) collective-permute-start(bf16[256,2048]{1,0:T(8,128)(2,1)S(1)} %dynamic-slice_bitcast_fusion.12), channel_id=1, source_target_pairs={{0,2},{1,3},{2,0},{3,1},{4,6},{5,7},{6,4},{7,5},{8,10},{9,11},{10,... | collective-permute-start | bytes 3145736 | tf_op jit(solution)/shard_map/cond/branch_1_fun/ppermute | solution.py:59
  944.4 38.6 %collective-permute-start.109 = (bf16[24,128,128]{2,1,0:T(8,128)(2,1)}, bf16[24,128,128]{2,1,0:T(8,128)(2,1)}, u32[]{:S(2)}, u32[]{:S(2)}) collective-permute-start(bf16[24,128,128]{2,1,0:T(8,128)(2,1)} %get-tuple-element.279), channel_id=1, source_target_pairs={{0,4},{4,0},{8,12},{12,8},{16,20},{20,16},{24,28},{28,24},{1,5},{5... | collective-permute-start | bytes 2359304 | tf_op jit(solution)/shard_map/cond/branch_1_fun/ppermute | solution.py:52
  950.0 80.9 %collective-permute-start.107 = (bf16[256,512]{1,0:T(8,128)(2,1)}, bf16[256,512]{1,0:T(8,128)(2,1)S(1)}, u32[]{:S(2)}, u32[]{:S(2)}) collective-permute-start(bf16[256,512]{1,0:T(8,128)(2,1)} %get-tuple-element.424), channel_id=1, source_target_pairs={{0,3},{1,0},{2,1},{3,2},{4,7},{5,4},{6,5},{7,6},{8,11},{9,8},{10,9... | collective-permute-start | bytes 786440 | tf_op jit(solution)/shard_map/cond/branch_1_fun/ppermute | solution.py:62
  982.9 60.7 %collective-permute-start.114 = (bf16[24,128,128]{2,1,0:T(8,128)(2,1)S(1)}, bf16[24,128,128]{2,1,0:T(8,128)(2,1)S(1)}, u32[]{:S(2)}, u32[]{:S(2)}) collective-permute-start(bf16[24,128,128]{2,1,0:T(8,128)(2,1)S(1)} %copy-done.108), channel_id=1, source_target_pairs={{0,4},{4,0},{8,12},{12,8},{16,20},{20,16},{24,28},{28,24},{1,5},{5... | collective-permute-start | bytes 2359304 | tf_op jit(solution)/shard_map/cond/branch_1_fun/ppermute | solution.py:52
  984.0 59.7 %collective-permute-start.113 = (bf16[24,128,128]{2,1,0:T(8,128)(2,1)}, bf16[24,128,128]{2,1,0:T(8,128)(2,1)S(1)}, u32[]{:S(2)}, u32[]{:S(2)}) collective-permute-start(bf16[24,128,128]{2,1,0:T(8,128)(2,1)} %fusion.56), channel_id=1, source_target_pairs={{0,24},{4,28},{8,0},{12,4},{16,8},{20,12},{24,16},{28,20},{1,25},{... | collective-permute-start | bytes 2359304 | tf_op jit(solution)/shard_map/cond/branch_1_fun/ppermute | solution.py:41
  986.1 57.6 %collective-permute-start.115 = (bf16[24,128,128]{2,1,0:T(8,128)(2,1)}, bf16[24,128,128]{2,1,0:T(8,128)(2,1)S(1)}, u32[]{:S(2)}, u32[]{:S(2)}) collective-permute-start(bf16[24,128,128]{2,1,0:T(8,128)(2,1)} %fusion.54), channel_id=1, source_target_pairs={{0,24},{4,28},{8,0},{12,4},{16,8},{20,12},{24,16},{28,20},{1,25},{... | collective-permute-start | bytes 2359304 | tf_op jit(solution)/shard_map/cond/branch_1_fun/ppermute | solution.py:41
  (140 other events, 2925.1 us)
Sparse Core Ops, SparseCore 0:
  28.9 36.1 all-gather.20
  148.7 89.2 all-gather.22
  239.7 70.5 all-gather.24
  311.8 79.3 all-gather.26
  392.7 33.0 all-gather.28
  631.9 44.2 reduce-scatter.16
  687.4 67.8 reduce-scatter.20
  800.8 47.4 reduce-scatter.18
  855.9 73.1 reduce-scatter.22

commit v2 on v1

--- a/solution.py
+++ b/solution.py
@@ -62,16 +62,16 @@
         return lax.ppermute(value, "tensor", [(i, (i + step) % self.n_t) for i in range(self.n_t)])
 
     def gather_rows(self, own, meanwhile=None):
-        rows = own.shape[0]
         pieces = [(self.y, own)]
         for step in range(1, self.ny):
-            pieces.append(((self.y + self.ny - step) % self.ny, self.shift_y(own, step)))
+            got = self.shift_y(own, step)
+            if meanwhile is not None and step == 1:
+                got = after(got, *meanwhile(own))
+            pieces.append(((self.y + self.ny - step) % self.ny, got))
         parts, places = [], []
         for row_y, piece in pieces:
             parts += [piece, self.swap_core(piece)]
             places += [2 * row_y + self.c, 2 * row_y + 1 - self.c]
-        if meanwhile is not None:
-            parts[-1] = after(parts[-1], *meanwhile(own))
         return stack_rows(parts, jnp.stack(places))
 
     def reduce_rows(self, part, meanwhile=None):
@@ -173,8 +173,8 @@
 
                 def step(k, carry, s=s, m=m, base=base, cols=cols, off=off, row=row, skip=lo - at):
                     tile = ids_ref[row, k] - base
-                    r = tile // cols
-                    c = tile - r * cols + off
+                    r = tile >> (cols.bit_length() - 1)
+                    c = (tile & (cols - 1)) + off
                     pltpu.make_async_copy(
                         refs[s].at[k - skip],
                         outs[m].at[
@@ -206,8 +206,10 @@
     )(ids, counts, *arrays)
 
 
-def pick_tiles(matrices, parts, ids, counts, rows, lo, hi, size_b):
-    n_src, n_out = len(matrices), len(rows)
+def pick_tiles(matrices, parts, ids, counts, rows, lo, hi, size_b, extra=None):
+    n_mat, n_out = len(matrices), len(rows)
+    more = [] if extra is None else [extra]
+    n_src = n_mat + len(more)
 
     def kernel(ids_ref, counts_ref, *refs):
         outs, sem = refs[n_src : n_src + n_out], refs[-1]
@@ -217,8 +219,8 @@
 
                     def step(k, carry, i=i, j=j, row=row, m=m, base=base, cols=cols, off=off):
                         tile = ids_ref[row, k] - base
-                        r = tile // cols
-                        c = tile - r * cols + off
+                        r = tile >> (cols.bit_length() - 1)
+                        c = (tile & (cols - 1)) + off
                         pltpu.make_async_copy(
                             refs[m].at[
                                 pl.ds(pl.multiple_of(r * size_b, size_b), size_b),
@@ -232,6 +234,10 @@
                     first = jnp.maximum(counts_ref[row, edge], lo)
                     last = jnp.minimum(counts_ref[row, edge + 1], hi)
                     lax.fori_loop(first, last, step, 0)
+        if more:
+            for i, group in enumerate(rows):
+                for j in range(len(group)):
+                    pltpu.make_async_copy(refs[n_mat], outs[i].at[j, hi - lo], sem).start()
         for out in outs:
             pltpu.make_async_copy(out, out, sem).wait()
 
@@ -244,10 +250,12 @@
             out_specs=[pl.BlockSpec(memory_space=pltpu.VMEM)] * n_out,
             scratch_shapes=[pltpu.SemaphoreType.DMA],
         ),
-        out_shape=[jax.ShapeDtypeStruct((len(group), hi - lo, size_b, size_b), bf16) for group in rows],
+        out_shape=[
+            jax.ShapeDtypeStruct((len(group), hi - lo + len(more), size_b, size_b), bf16) for group in rows
+        ],
         compiler_params=pltpu.CompilerParams(vmem_limit_bytes=60 * MIB),
         name="pick_tiles",
-    )(ids, counts, *matrices)
+    )(ids, counts, *matrices, *more)
 
 
 def dot_nt(a, b):
@@ -260,6 +268,76 @@
 
 def dot_nn(a, b):
     return lax.dot_general(a, b, (((1,), (0,)), ((), ())), preferred_element_type=f32)
+
+
+def kept(shape):
+    return pl.BlockSpec(shape, lambda i: (0,) * len(shape), pipeline_mode=pl.Buffered(1))
+
+
+ROOMY = pltpu.CompilerParams(vmem_limit_bytes=52 * MIB)
+
+
+def product_tn(a, b):
+    (rows, m), n = a.shape, b.shape[1]
+    step = min(512, m)
+
+    def kernel(a_ref, b_ref, out_ref):
+        out_ref[...] = dot_tn(a_ref[...], b_ref[...]).astype(bf16)
+
+    return pl.pallas_call(
+        kernel,
+        grid=(m // step,),
+        in_specs=[pl.BlockSpec((rows, step), lambda i: (0, i)), kept((rows, n))],
+        out_specs=pl.BlockSpec((step, n), lambda i: (i, 0)),
+        out_shape=jax.ShapeDtypeStruct((m, n), bf16),
+        compiler_params=ROOMY,
+        name="product_tn",
+    )(a, b)
+
+
+def product_nt(*pairs):
+    count, rows, n = len(pairs), pairs[0][0].shape[0], pairs[0][1].shape[0]
+    step = min(256, n)
+
+    def kernel(*refs):
+        total = dot_nt(refs[0][...], refs[count][...])
+        for i in range(1, count):
+            total = total + dot_nt(refs[i][...], refs[count + i][...])
+        refs[-1][...] = total.astype(bf16)
+
+    return pl.pallas_call(
+        kernel,
+        grid=(n // step,),
+        in_specs=[kept(a.shape) for a, _ in pairs]
+        + [pl.BlockSpec((step, b.shape[1]), lambda i: (i, 0)) for _, b in pairs],
+        out_specs=pl.BlockSpec((rows, step), lambda i: (0, i)),
+        out_shape=jax.ShapeDtypeStruct((rows, n), bf16),
+        compiler_params=ROOMY,
+        name="product_nt",
+    )(*[a for a, _ in pairs], *[b for _, b in pairs])
+
+
+def inner_back(d_mlp, w_down, gate_act, up_act):
+    rows, hidden = gate_act.shape
+    step = min(512, hidden)
+
+    def kernel(d_ref, w_ref, gate_ref, up_ref, d_gate_ref, d_up_ref):
+        d_inner = dot_nt(d_ref[...], w_ref[...])
+        gate = gate_ref[...]
+        sig = jax.nn.sigmoid(gate)
+        d_gate_ref[...] = (d_inner * up_ref[...] * sig * (1.0 + gate * (1.0 - sig))).astype(bf16)
+        d_up_ref[...] = (d_inner * (gate * sig)).astype(bf16)
+
+    strip = pl.BlockSpec((rows, step), lambda i: (0, i))
+    return pl.pallas_call(
+        kernel,
+        grid=(hidden // step,),
+        in_specs=[kept(d_mlp.shape), pl.BlockSpec((step, w_down.shape[1]), lambda i: (i, 0)), strip, strip],
+        out_specs=[strip, strip],
+        out_shape=[jax.ShapeDtypeStruct((rows, hidden), bf16)] * 2,
+        compiler_params=ROOMY,
+        name="inner_back",
+    )(d_mlp, w_down, gate_act, up_act)
 
 
 def softmax_block(q_block, k_head, first, length):
@@ -356,15 +434,16 @@
     )(lengths, q_low, k_low, v_low, d_attn, cos_t, sin_t)
 
 
-def renew(grads, perm, lo, held, outs):
+def renew(grads, perm, lo, held, outs, fetched=None):
     count, size_b = grads.shape[0], grads.shape[-1]
     n_old = 0 if outs is None else len(outs)
     batch = fit(count)
     steps = count // batch
 
+    n_in = 5 * batch if fetched is None else 1
+
     def kernel(perm_ref, g_ref, *refs):
-        ins = [refs[a * batch : (a + 1) * batch] for a in range(5)]
-        outs_ref = refs[5 * batch + n_old : 5 * batch + n_old + 4]
+        outs_ref = refs[n_in + n_old : n_in + n_old + 4]
         held_ref, sems = refs[-2:]
         i = pl.program_id(0)
         side = i % 2
@@ -377,7 +456,11 @@
             drain(side)
 
         for j in range(batch):
-            master, left_s, right_s, left_r, right_r = (ins[a][j][0] for a in range(5))
+            if fetched is None:
+                tiles = [refs[a * batch + j][0] for a in range(5)]
+            else:
+                tiles = [refs[0][j, a] for a in range(5)]
+            master, left_s, right_s, left_r, right_r = tiles
             g = g_ref[j]
             held_ref[side, 0, j] = g.astype(f32)
             held_ref[side, 1, j] = DECAY * left_s + (1.0 - DECAY) * dot_nt(g, g)
@@ -404,7 +487,11 @@
             num_scalar_prefetch=1,
             grid=(steps,),
             in_specs=[pl.BlockSpec((batch, size_b, size_b), lambda i, p: (i, 0, 0))]
-            + [spec(j) for _ in range(5) for j in range(batch)]
+            + (
+                [spec(j) for _ in range(5) for j in range(batch)]
+                if fetched is None
+                else [pl.BlockSpec((batch, 5, size_b, size_b), lambda i, p: (lo // batch + i, 0, 0, 0))]
+            )
             + [pl.BlockSpec(memory_space=pl.ANY)] * n_old,
             out_specs=[pl.BlockSpec(memory_space=pl.ANY)] * 4,
             scratch_shapes=[
@@ -413,9 +500,40 @@
             ],
         ),
         out_shape=[jax.ShapeDtypeStruct(held[0].shape, f32)] * 4,
-        input_output_aliases={2 + 5 * batch + i: i for i in range(n_old)},
+        input_output_aliases={2 + n_in + i: i for i in range(n_old)},
+        compiler_params=pltpu.CompilerParams(vmem_limit_bytes=40 * MIB),
         name="renew",
-    )(perm, grads, *[array for array in held for _ in range(batch)], *(outs or ()))
+    )(perm, grads, *([array for array in held for _ in range(batch)] if fetched is None else [fetched]), *(outs or ()))
+
+
+def fetch(perm, count, held):
+    size_b = held[0].shape[-1]
+
+    def kernel(perm_ref, *refs):
+        out, sem = refs[-2:]
+
+        def step(k, carry):
+            slot = perm_ref[k]
+            for a in range(5):
+                pltpu.make_async_copy(refs[a].at[slot], out.at[k, a], sem).start()
+            return carry
+
+        lax.fori_loop(0, count, step, 0)
+        pltpu.make_async_copy(out, out, sem).wait()
+
+    return pl.pallas_call(
+        kernel,
+        grid_spec=pltpu.PrefetchScalarGridSpec(
+            num_scalar_prefetch=1,
+            grid=(1,),
+            in_specs=[pl.BlockSpec(memory_space=pl.ANY)] * 5,
+            out_specs=pl.BlockSpec(memory_space=pltpu.VMEM),
+            scratch_shapes=[pltpu.SemaphoreType.DMA],
+        ),
+        out_shape=jax.ShapeDtypeStruct((count, 5, size_b, size_b), f32),
+        compiler_params=pltpu.CompilerParams(vmem_limit_bytes=40 * MIB),
+        name="fetch",
+    )(perm, *held)
 
 
 def rope_tables(seq_len):
@@ -426,7 +544,16 @@
     return jnp.concatenate([cos_t, cos_t], 1), jnp.concatenate([-sin_t, sin_t], 1)
 
 
-def core(fast, cuts, links, tables, perm, gain_full, args):
+def gather_front(links, cuts, tokens, master, perm):
+    edge_a, edge_b1, edge_b, count = cuts["a"], cuts["b1"], cuts["b"], cuts["end"]
+    own_a = sorted_tiles(master, perm, 0, edge_a)
+    later = after(perm, own_a)
+    owns = [sorted_tiles(master, later, lo, hi) for lo, hi in ((edge_a, edge_b1), (edge_b1, edge_b), (edge_b, count))]
+    tok_full = lax.all_gather(tokens, "tensor", axis=1, tiled=True)
+    return owns, own_a, links.swap_x(own_a), links.ring(own_a), tok_full
+
+
+def core(fast, cuts, links, tables, perm, gain_full, front, args):
     tokens, cotangent, lengths, gains, gain_stats, gain_roots = args[:6]
     master, left_stats, right_stats, left_roots, right_roots = args[6:]
     ids, counts = tables
@@ -444,24 +571,16 @@
     )
 
     edge_a, edge_b1, edge_b, count = cuts["a"], cuts["b1"], cuts["b"], cuts["end"]
-    own_a = sorted_tiles(master, perm, 0, edge_a)
-    later = after(perm, own_a)
-    owns = [sorted_tiles(master, later, lo, hi) for lo, hi in ((edge_a, edge_b1), (edge_b1, edge_b), (edge_b, count))]
-    tok_full = lax.all_gather(tokens, "tensor", axis=1, tiled=True)
-    cot_full = lax.all_gather(cotangent, "tensor", axis=1, tiled=True)
-
-    mine, theirs = [own_a], [links.swap_x(own_a)]
-    for r in range(1, links.nz):
-        if r == 1:
-            mine.append(links.ring(own_a))
-        else:
-            mine.append(links.ring(after(mine[-1], theirs[r - 2], *(owns if r == 2 else ()))))
-        if r > 1:
-            theirs.append(links.swap_x(after(mine[r - 1], theirs[-1])))
+    owns, own_a, their_a, next_a, tok_full = front
+    mine, theirs = [own_a, next_a], [their_a]
+    for r in range(2, links.nz):
+        mine.append(links.ring(after(mine[-1], theirs[r - 2])))
+        theirs.append(links.swap_x(after(mine[r - 1], theirs[-1])))
     theirs.append(links.swap_x(after(mine[-1], theirs[-1])))
     own_b1 = links.swap_x(after(owns[0], theirs[-1]))
     own_c = links.swap_x(after(owns[2], own_b1))
     own_b2 = links.swap_x(after(owns[1], own_b1))
+    cot_full = lax.all_gather(cotangent, "tensor", axis=1, tiled=True)
     sources_a = []
     for r in range(links.nz):
         sources_a.append((mine[r], 0, 2 * r, 0, edge_a))
@@ -470,10 +589,14 @@
     def matrices(sources, groups, shapes):
         return place_tiles(sources, [(m,) + part for m, part in groups], shapes, ids, counts, size_b)
 
-    def send_others(gathered, n, last):
+    def others(gathered, n):
+        return [
+            lax.dynamic_slice_in_dim(gathered, ((links.z + r) % links.nz) * n, n, 0) for r in range(1, links.nz)
+        ]
+
+    def send_others(pieces, last):
         sent = []
-        for r in range(1, links.nz):
-            piece = lax.dynamic_slice_in_dim(gathered, ((links.z + r) % links.nz) * n, n, 0)
+        for piece in pieces:
             last = links.swap_x(after(piece, last))
             sent.append(last)
         return sent
@@ -488,8 +611,9 @@
     z_b1, z_b2, z_c = (
         links.gather_z(after(own, mine[-1], theirs[-2])) for own in (owns[0], owns[1], jnp.concatenate([owns[2], own_c], axis=0))
     )
-    rest_b1 = send_others(z_b1, n_b1, own_b2)
-    rest_b2 = send_others(z_b2, n_b2, rest_b1[-1])
+    pieces_b1 = others(z_b1, n_b1)
+    rest_b1 = send_others(pieces_b1, own_b2)
+    rest_b2 = send_others(others(z_b2, n_b2), rest_b1[-1])
     sources_b1 = sources_a + all_sources(edge_a, edge_b1, z_b1, own_b1, rest_b1)
     sources_b2 = sources_b1 + all_sources(edge_b1, edge_b, z_b2, own_b2, rest_b2)
     sources_c = sources_b2 + [
@@ -520,8 +644,7 @@
     scale_q = lax.rsqrt(squares[0] / width_d + EPSILON)[:, None]
     scale_k = lax.rsqrt(squares[1] / width_d + EPSILON)[:, None]
     attn_low, q_low, k_low, v_low = attention(raw, scale_q, scale_k, gain_local, cos_t, sin_t, lengths)
-    branch = links.reduce_rows(dot_nn(after(attn_low, own_c, own_b2), w_o).astype(bf16))
-    branch = after(branch, z_b1)
+    branch = links.reduce_rows(dot_nn(after(attn_low, own_c, own_b2, pieces_b1[0]), w_o).astype(bf16))
     rms_a = lax.rsqrt(jnp.mean(branch * branch, axis=-1, keepdims=True) + EPSILON)
     hidden_rows = tok_rows + branch * rms_a * gain_full[2]
     hidden_low = links.gather_rows(hidden_rows.astype(bf16))
@@ -546,15 +669,14 @@
     grads = {}
     grad_parts = [(0, down_part), (1, up_part), (2, gate_part), (3, o_part)] + [(4, p) for p in qkv_parts]
     held = (master, left_stats, right_stats, left_roots, right_roots)
+    edge_m = (edge_a + edge_b1) // 4 * 2
+    rows_x = [[links.n_dp + 2 * z + xr for z in range(links.nz)] for xr in (1, 0)]
     half_z = links.nz // 2
-    edge_m = (edge_a + edge_b1) // 4 * 2
-    abs_row = lambda z, xr: links.n_dp + 2 * z + xr
-    theirs_rows = [[abs_row(z, 1) for z in range(half_z)], [abs_row(z, 1) for z in range(half_z, links.nz)]]
-    mine_rows = [abs_row(z, 0) for z in range(links.nz)]
-
-    def cut_out(lo, hi, n_mats, rows):
+    rows_halves = [rows_x[0][:half_z], rows_x[0][half_z:], rows_x[1]]
+
+    def cut_out(lo, hi, n_mats, rows, extra=None):
         parts = [(m,) + part for m, part in grad_parts if m < n_mats]
-        return pick_tiles([grads[m] for m in range(n_mats)], parts, ids, counts, rows, lo, hi, size_b)
+        return pick_tiles([grads[m] for m in range(n_mats)], parts, ids, counts, rows, lo, hi, size_b, extra)
 
     def flat(value):
         return value.reshape((-1, size_b, size_b))
@@ -562,38 +684,32 @@
     def summed(mine, *got):
         return (flat(mine).astype(f32) + jnp.concatenate(got, axis=0).astype(f32)).astype(bf16)
 
-    full_rows = theirs_rows + [mine_rows]
-    grads[0] = dot_tn(inner_low, d_mlp_low).astype(bf16)
+    grads[0] = product_tn(inner_low, d_mlp_low)
     if fast:
-        out_a, out_b, mine_0 = cut_out(edge_b, count, 1, full_rows)
-        got_0a = links.swap_x(flat(out_a))
-        got_0b = links.swap_x(after(flat(out_b), got_0a))
-        d_mlp_low = after(d_mlp_low, out_a)
-    d_inner = dot_nt(d_mlp_low, w_down)
-    d_gate = (d_inner * up_act * sig_gate * (1.0 + gate_act * (1.0 - sig_gate))).astype(bf16)
-    d_up = (d_inner * silu_act).astype(bf16)
+        out_0, mine_0 = cut_out(edge_b, count, 1, rows_x)
+        got_0 = links.swap_x(flat(out_0))
+        d_mlp_low = after(d_mlp_low, out_0)
+    d_gate, d_up = inner_back(d_mlp_low, w_down, gate_act, up_act)
+    grads[1] = product_tn(hidden_low, d_up)
     if fast:
-        d_up, d_gate = lax.optimization_barrier((d_up, d_gate, got_0a))[:2]
-    grads[1] = dot_tn(hidden_low, d_up).astype(bf16)
-    if fast:
-        out_a, out_b, mine_1 = cut_out(edge_b1, edge_b, 2, full_rows)
-        total_0 = links.reduce_z(summed(mine_0, got_0a, after(got_0b, out_a)))
-        got_1a = links.swap_x(after(flat(out_a), got_0b))
-        got_1b = links.swap_x(after(flat(out_b), got_1a))
-        d_gate = after(d_gate, out_a, got_0b)
-    grads[2] = dot_tn(hidden_low, d_gate).astype(bf16)
+        out_1a, out_1b, mine_1 = cut_out(edge_b1, edge_b, 2, rows_halves)
+        sum_0 = summed(mine_0, after(got_0, out_1a))
+        total_0 = links.reduce_z(sum_0)
+        got_1a = links.swap_x(after(flat(out_1a), got_0))
+        got_1b = links.swap_x(after(flat(out_1b), got_1a))
+        d_gate = after(d_gate, sum_0)
+    grads[2] = product_tn(hidden_low, d_gate)
     d_up_in = after(d_up, grads[2])
-    back_part = (dot_nt(d_gate, w_gate) + dot_nt(d_up_in, w_up)).astype(bf16)
+    back_part = product_nt((d_gate, w_gate), (d_up_in, w_up))
     if fast:
         back_part = after(back_part, got_1a)
     sends = {}
-    both_x = [theirs_rows[0] + theirs_rows[1], mine_rows]
 
     def while_reducing(both):
         grads[2] = after(grads[2], both)
-        sends["2a"] = cut_out(edge_m, edge_b1, 3, both_x)
-        sends["2b"] = cut_out(edge_a, edge_m, 3, both_x)
-        return (sends["2b"][0],)
+        sends["2a"] = cut_out(edge_m, edge_b1, 3, rows_x)
+        sends["2b"] = cut_out(edge_a, edge_m, 3, rows_x)
+        return (sends["2a"][0], sends["2b"][0], total_0)
 
     def while_gathering(own):
         sum_1 = summed(mine_1, got_1a, after(got_1b, own))
@@ -608,13 +724,14 @@
     scaled_a = gain_full[2] * d_hidden
     d_branch = rms_a * scaled_a - branch * rms_a**3 * jnp.mean(scaled_a * branch, axis=-1, keepdims=True)
     d_branch_low = links.gather_rows(d_branch.astype(bf16), while_gathering if fast else None)
-    d_attn = dot_nt(d_branch_low, w_o).astype(bf16)
+    d_attn = product_nt((d_branch_low, w_o))
     if fast:
-        sum_2a = summed(sends["2a"][1], after(got_2a, d_attn))
-        total_2a = links.reduce_z(sum_2a)
-        d_attn = after(d_attn, sum_2a)
         total_1, outs = sends["1"], sends["outs"]
     d_qn, d_kn, d_values = attention_back(q_low, k_low, v_low, d_attn, cos_t, sin_t, lengths)
+    if fast:
+        sum_2a = summed(sends["2a"][1], after(got_2a, d_qn))
+        total_2a = links.reduce_z(sum_2a)
+        d_qn = after(d_qn, sum_2a, total_1)
     scaled_q = gain_local[0] * d_qn
     scaled_k = gain_local[1] * d_kn
     gain_m_all = jnp.sum(grad_rows * mlp_rows * rms_m, axis=0)
@@ -635,75 +752,16 @@
     d_queries = scale_q * scaled_q - queries * scale_q**3 * (stat_q / width_d)[:, None]
     d_keys = scale_k * scaled_k - keys_raw * scale_k**3 * (stat_k / width_d)[:, None]
     d_qkv = jnp.concatenate([d_queries.astype(bf16), d_keys.astype(bf16), d_values], axis=1)
-    grads[4] = dot_tn(tok_full, d_qkv).astype(bf16)
-    grads[3] = dot_tn(attn_low, d_branch_low).astype(bf16)
+    grads[4] = product_tn(tok_full, d_qkv)
+    grads[3] = product_tn(attn_low, d_branch_low)
     if not fast:
         totals = []
         for lo, hi in ((edge_b, count), (edge_b1, edge_b), (edge_m, edge_b1), (edge_a, edge_m)):
-            out_a, out_b, mine_n = cut_out(lo, hi, 5, full_rows)
-            got_2a, got_2b = links.swap_x(flat(out_a)), links.swap_x(flat(out_b))
-            totals.append(links.reduce_z(summed(mine_n, got_2a, got_2b)))
+            out_n, mine_n = cut_out(lo, hi, 5, rows_x)
+            got_2a = got_2b = links.swap_x(flat(out_n))
+            totals.append(links.reduce_z(summed(mine_n, got_2a)))
         total_0, total_1, total_2a, total_2b = totals
         outs = renew(total_0, perm, edge_b, held, None)
-
-    mid = edge_a // 4 * 2
-    turns = list(range(1, links.nz)) + [0]
-    first_cut = cut_out(0, edge_a, 5, [[2 * turns[0] + 1], [2 * turns[0]]])
-    grads[4] = after(grads[4], first_cut[0])
-    rest = cut_out(0, edge_a, 5, [[2 * r + 1] for r in turns[1:]] + [[2 * r for r in turns[1:]]])
-    to_send = [first_cut[0][0]] + [rest[k][0] for k in range(links.nz - 1)]
-    to_keep = [first_cut[1][0]] + [rest[-1][k] for k in range(links.nz - 1)]
-    pins = (rest[0],)
-    late = [(edge_b1, total_1), (edge_m, total_2a), (edge_a, total_2b)] if not fast else []
-    if fast:
-        sum_2b = summed(sends["2b"][1], after(got_2b, rest[0]))
-        total_2b = links.reduce_z(sum_2b)
-        pins = (rest[0], sum_2b)
-        late = [(edge_b1, total_1), (edge_m, total_2a), (edge_a, total_2b)]
-
-    def joined(kept, got, ring):
-        total = kept.astype(f32) + got.astype(f32)
-        if ring is not None:
-            total = total + ring.astype(f32)
-        return total.astype(bf16)
-
-    x_done = [got_2a, got_2b]
-    ring = None
-    for event in range(links.nz - 2):
-        got = links.swap_x(after(to_send[event], x_done[-2]))
-        x_done.append(got)
-        total = joined(to_keep[event], after(got, *pins), ring)
-        ring = links.ring(total)
-        if event == 0:
-            input_part = dot_nt(after(d_qkv, total), w_qkv).astype(bf16)
-            pins = (input_part,)
-        elif late:
-            lo, ready = late.pop(0)
-            outs = renew(after(ready, total), perm, lo, held, outs)
-            pins = (outs[0],)
-    halves = ((0, mid), (mid, edge_a))
-    last_rings = []
-    for lo, hi in halves:
-        got = links.swap_x(after(to_send[-2][lo:hi], x_done[-2]))
-        x_done.append(got)
-        total = joined(to_keep[-2][lo:hi], after(got, *pins), ring[lo:hi])
-        last_rings.append(links.ring(total))
-        pins = ()
-        if late:
-            at, ready = late.pop(0)
-            outs = renew(after(ready, total), perm, at, held, outs)
-            pins = (outs[0],)
-    gain_start = total
-    for (lo, hi), ring in zip(halves, last_rings):
-        got = links.swap_x(after(to_send[-1][lo:hi], x_done[-2]))
-        x_done.append(got)
-        total = joined(to_keep[-1][lo:hi], after(got, *pins), ring)
-        pins = ()
-        outs = renew(total, perm, lo, held, outs)
-
-    input_rows = links.reduce_rows(input_part)
-    token_grads = links.rows_to_cols((input_rows + d_hidden).astype(bf16))
-    block_out = links.rows_to_cols(after(result, x_done[3]).astype(bf16))
 
     gain_terms = jnp.stack(
         [
@@ -713,12 +771,73 @@
             lax.dynamic_slice_in_dim(gain_m_all, links.t * width_local, width_local, 0),
         ]
     )
-    gain_terms = after(gain_terms, gain_start)
-    gain_part = gain_terms + links.swap_x(gain_terms)
-    gain_grads = gain_part
-    for r in range(1, links.nz):
-        gain_part = links.ring(gain_part)
-        gain_grads = gain_grads + gain_part
+    gain_lines = gain_terms.size // size_b
+    gain_slot = jnp.pad(gain_terms.reshape(gain_lines, size_b), ((0, size_b - gain_lines), (0, 0))).astype(bf16)
+    mid = edge_a // 4 * 2
+    turns = list(range(1, links.nz)) + [0]
+    first_cut = cut_out(0, edge_a, 5, [[2 * turns[0] + 1], [2 * turns[0]]], gain_slot)
+    grads[4] = after(grads[4], first_cut[0])
+    rest_rows = [[2 * r + 1] for r in turns[1:]] + [[2 * r for r in turns[1:]]]
+    rest = cut_out(0, edge_a, 5, rest_rows, gain_slot)
+    rest = list(rest)
+    if fast:
+        rest[0] = after(rest[0], total_2a)
+    to_send = [first_cut[0][0]] + [rest[k][0] for k in range(links.nz - 1)]
+    to_keep = [first_cut[1][0]] + [rest[-1][k] for k in range(links.nz - 1)]
+    pins = (rest[0],)
+    if fast:
+        sum_2b = summed(sends["2b"][1], after(got_2b, rest[0]))
+        total_2b = links.reduce_z(sum_2b)
+        pins = (rest[0], sum_2b)
+    outs = renew(total_1, perm, edge_b1, held, outs)
+    outs = renew(total_2a, perm, edge_m, held, outs)
+    to_send[1] = after(to_send[1], outs[0])
+
+    def joined(kept, got, ring, pins):
+        got = after(got, *pins)
+        total = kept.astype(f32) + got.astype(f32)
+        if ring is not None:
+            total = total + after(ring, *pins).astype(f32)
+        return total.astype(bf16)
+
+    x_done = [got_2a, got_2b]
+    ring = None
+    for event in range(links.nz - 2):
+        got = links.swap_x(after(to_send[event], x_done[-2]))
+        x_done.append(got)
+        total = joined(to_keep[event], got, ring, pins)
+        ring = links.ring(total)
+        pins = ()
+        if event == 0:
+            input_part = product_nt((after(d_qkv, total), w_qkv))
+            pins = (input_part, total_2b)
+        if event == links.nz - 3:
+            total_at_1 = total
+    halves = ((0, mid), (mid, edge_a + 1))
+    last_rings = []
+    outs = renew(total_2b, perm, edge_a, held, outs)
+    to_send[-2] = after(to_send[-2], outs[0])
+    fetched = fetch(after(perm, total), edge_a, held)
+    to_send[-1] = after(to_send[-1], fetched)
+    for lo, hi in halves:
+        got = links.swap_x(after(to_send[-2][lo:hi], x_done[-2]))
+        x_done.append(got)
+        total = joined(to_keep[-2][lo:hi], got, ring[lo:hi], pins)
+        last_rings.append(links.ring(total))
+        pins = ()
+    for (lo, hi), ring in zip(halves, last_rings):
+        got = links.swap_x(after(to_send[-1][lo:hi], x_done[-2]))
+        x_done.append(got)
+        n = min(hi, edge_a) - lo
+        total = joined(to_keep[-1][lo : lo + n], got[:n], ring[:n], ())
+        outs = renew(total, perm, lo, held, outs, fetched)
+    gain_grads = joined(to_keep[-1][edge_a], got[-1], ring[-1], ()).astype(f32)
+    gain_grads = gain_grads[:gain_lines].reshape(gain_terms.shape)
+
+    input_rows = links.reduce_rows(after(input_part, total_at_1))
+    token_grads = links.rows_to_cols((input_rows + d_hidden).astype(bf16))
+    block_out = links.rows_to_cols(after(result, x_done[3]).astype(bf16))
+
     gain_stats_new = DECAY * gain_stats + (1.0 - DECAY) * gain_grads * gain_grads
     gains_new = gains - GAIN_RATE * gain_grads * gain_roots
 
@@ -796,8 +915,10 @@
     args = (tokens, cotangent, lengths, gains, gain_stats, gain_roots)
     args = args + (master[0], left_stats[0], right_stats[0], left_roots[0], right_roots[0])
 
+    front = gather_front(links, cuts, tokens, master[0], perm)
+
     def run(fast):
-        return lambda *rest: core(fast, cuts, links, tables, perm, gain_full, rest)
+        return lambda *rest: core(fast, cuts, links, tables, perm, gain_full, front, rest)
 
     if MODE == "fast":
         return run(True)(*args)

time: 1080 us -> 1020 us (0.944)
  Pallas kernels: 199 us -> 317 us
  matrix products: 163 us -> 48.8 us
  waiting for transfers between devices: 462 us -> 415 us
  other arithmetic: 81.6 us -> 70.1 us
    pallas_call x0 -> x10, Pallas kernels: none -> 129 us  [the longest x5 56.7 us: product_tn(): pl.pallas_call(kernel, grid=(m // step,), in_specs=[pl.BlockSpec((rows, s...]
    dot_general x10 -> x0, matrix products: 111 us -> none  [the longest x5 58.8 us: dot_nt(): lax.dot_general(a, b, (((1,), (1,)), ((), ())), preferred_element_type=f32)]
    ppermute x26 -> x24, waiting for transfers between devices: 267 us -> 214 us  [swap_x(): return lax.ppermute(value, 'dp', [(i, i ^ 1) for i in range(self.n_dp)])]
    ppermute x10 -> x7, waiting for transfers between devices: 118 us -> 98.3 us  [ring(): return lax.ppermute(value, 'dp', pairs)]
    ppermute x7, waiting for transfers between devices: 61.2 us -> 78.5 us  [shift_y(): return lax.ppermute(value, 'tensor', pairs)]
    ppermute x10 -> x7, starting transfers between devices: 25.1 us -> 16.9 us  [ring(): return lax.ppermute(value, 'dp', pairs)]
    ppermute x26 -> x24, starting transfers between devices: 30.8 us -> 29.5 us  [swap_x(): return lax.ppermute(value, 'dp', [(i, i ^ 1) for i in range(self.n_dp)])]
  transfers between devices with their start and end apart: 68 -> 63, of which waited for: 32 -> 35; matrix products, arithmetic and copies ran while one was open for 23% -> 12% of each run, Pallas kernels for 16% -> 29%
where the time goes in v2:
time: 1020 us; the launch traced here: 1010 us
  waiting for transfers between devices  415 us (41%)
  Pallas kernels  317 us (31%)
  other arithmetic  70.1 us (7%)
  starting transfers between devices  62.5 us (6%)
  matrix products  48.8 us (5%)
  local copies, waits for them, and re-layouts  47.7 us (5%)
  blocking collectives  23.4 us (2%)
  between operations  17.2 us (2%)
    ppermute x24, waiting for transfers between devices, swap_x(): return lax.ppermute(value, 'dp', [(i, i ^ 1) for i in range(self.n_dp)])  214 us
    ppermute x7, waiting for transfers between devices, ring(): return lax.ppermute(value, 'dp', pairs)  98.3 us
    ppermute x7, waiting for transfers between devices, shift_y(): return lax.ppermute(value, 'tensor', pairs)  78.5 us
    pallas_call x6, Pallas kernels, renew(): pl.pallas_call(kernel, grid_spec=pltpu.PrefetchScalarGridSpec(num_scalar_...  59.4 us
    pallas_call x5, Pallas kernels, product_tn(): pl.pallas_call(kernel, grid=(m // step,), in_specs=[pl.BlockSpec((rows, s...  56.7 us
    dot_general x5, matrix products, dot_nn(): lax.dot_general(a, b, (((1,), (0,)), ((), ())), preferred_element_type=f32)  48.8 us
    pallas_call x3, Pallas kernels, product_nt(): pl.pallas_call(kernel, grid=(n // step,), in_specs=[kept(a.shape) for a,...  41.6 us
    pallas_call x6, Pallas kernels, pick_tiles(): pl.pallas_call(kernel, grid_spec=pltpu.PrefetchScalarGridSpec(num_scalar_...  38.1 us
  transfers between devices with their start and end apart: 63, of which 35 were waited for; matrix products, arithmetic and copies ran while one was open for 12% of the time, Pallas kernels for 29%

profile of v2, /device:TPU:0, one launch (start us, length us, event | category | flops | bytes accessed | tf_op | source)
XLA Modules:
  0.0 1008.2 jit_solution(5738239082269501179)
XLA Ops:
  54.2 946.4 %conditional.1 = (bf16[1024,512]{1,0:T(8,128)(2,1)}, bf16[1024,512]{1,0:T(8,128)(2,1)}, f32[1,128,128,128]{3,2,1,0:T(8,128)}, f32[1,128,128,128]{3,2,1,0:T(8,128...) conditional(s32[]{:T(128)} %convert_element_type.588, ...), branch_computations={%region_6.25_spmd, %region_25.44_spmd} | conditional | flops 34508578816 | bytes 1240894208 | solution.py:925
  64.8 32.2 %collective-permute-done.52.refs_4_ = bf16[48,128,128]{2,1,0:T(8,128)(2,1)S(1)} collective-permute-done((bf16[48,128,128]{2,1,0:T(8,128)(2,1)}, bf16[48,128,128]{2,1,0:T(8,128)(2,1)S(1)}, u32[]{:S(2)}, u32[]{:S(2)}) %collective-permute-start.52) | collective-permute-done | bytes 1572896 | tf_op jit(solution)/shard_map/cond/branch_1_fun/ppermute | solution.py:41
  101.8 31.1 %collective-permute-done.54.refs_6_ = bf16[48,128,128]{2,1,0:T(8,128)(2,1)S(1)} collective-permute-done((bf16[48,128,128]{2,1,0:T(8,128)(2,1)S(1)}, bf16[48,128,128]{2,1,0:T(8,128)(2,1)S(1)}, u32[]{:S(2)}, u32[]{:S(2)}) %collective-permute-start.54) | collective-permute-done | bytes 1572896 | tf_op jit(solution)/shard_map/cond/branch_1_fun/ppermute | solution.py:41
  137.0 33.9 %collective-permute-done.55.refs_7_ = bf16[48,128,128]{2,1,0:T(8,128)(2,1)} collective-permute-done((bf16[48,128,128]{2,1,0:T(8,128)(2,1)}, bf16[48,128,128]{2,1,0:T(8,128)(2,1)}, u32[]{:S(2)}, u32[]{:S(2)}) %collective-permute-start.55) | collective-permute-done | bytes 1572896 | tf_op jit(solution)/shard_map/cond/branch_1_fun/ppermute | solution.py:52
  182.1 14.9 %collective-permute-done.56.refs_9_ = bf16[36,128,128]{2,1,0:T(8,128)(2,1)} collective-permute-done((bf16[36,128,128]{2,1,0:T(8,128)(2,1)}, bf16[36,128,128]{2,1,0:T(8,128)(2,1)}, u32[]{:S(2)}, u32[]{:S(2)}) %collective-permute-start.56) | collective-permute-done | bytes 1179680 | tf_op jit(solution)/shard_map/cond/branch_1_fun/ppermute | solution.py:52
  217.4 16.2 %attention.3 = (bf16[1024,512]{1,0:T(8,128)(2,1)S(1)}, bf16[1024,512]{1,0:T(8,128)(2,1)S(1)}, bf16[1024,512]{1,0:T(8,128)(2,1)S(1)}, bf16[1024,512]{1,0:T(8,128)(2,1)}) custom-call(s32[1]{0:T(128)} %get-tuple-element.213.len_ref, f32[1024,1536]{1,0:T(8,128)} %copy-done.32, f32[1024,1536]{1,0:T(8,128)} %copy-done.32, f32[1024,1536]{1,0:T(8,128)} %copy-done.32, ...), custom_call_target="tpu_custom_call" | custom-call | tf_op jit(solution)/shard_map/cond/branch_1_fun/attention/pallas_call | solution.py:376
  248.7 27.1 %collective-permute-done.64.refs_10_ = bf16[36,128,128]{2,1,0:T(8,128)(2,1)S(1)} collective-permute-done((bf16[36,128,128]{2,1,0:T(8,128)(2,1)}, bf16[36,128,128]{2,1,0:T(8,128)(2,1)S(1)}, u32[]{:S(2)}, u32[]{:S(2)}) %collective-permute-start.64) | collective-permute-done | bytes 1179680 | tf_op jit(solution)/shard_map/cond/branch_1_fun/ppermute | solution.py:52
  284.2 19.5 %collective-permute-done.65.refs_11_ = bf16[36,128,128]{2,1,0:T(8,128)(2,1)} collective-permute-done((bf16[36,128,128]{2,1,0:T(8,128)(2,1)}, bf16[36,128,128]{2,1,0:T(8,128)(2,1)}, u32[]{:S(2)}, u32[]{:S(2)}) %collective-permute-start.65) | collective-permute-done | bytes 1179680 | tf_op jit(solution)/shard_map/cond/branch_1_fun/ppermute | solution.py:52
  317.3 13.6 %collective-permute-done.66.refs_12_ = bf16[36,128,128]{2,1,0:T(8,128)(2,1)} collective-permute-done((bf16[36,128,128]{2,1,0:T(8,128)(2,1)}, bf16[36,128,128]{2,1,0:T(8,128)(2,1)}, u32[]{:S(2)}, u32[]{:S(2)}) %collective-permute-start.66) | collective-permute-done | bytes 1179680 | tf_op jit(solution)/shard_map/cond/branch_1_fun/ppermute | solution.py:52
  336.3 15.0 %collective-permute-done.67.refs_15_ = bf16[28,128,128]{2,1,0:T(8,128)(2,1)} collective-permute-done((bf16[28,128,128]{2,1,0:T(8,128)(2,1)S(1)}, bf16[28,128,128]{2,1,0:T(8,128)(2,1)}, u32[]{:S(2)}, u32[]{:S(2)}) %collective-permute-start.67) | collective-permute-done | bytes 917536 | tf_op jit(solution)/shard_map/cond/branch_1_fun/ppermute | solution.py:52
  408.1 16.4 %multiply_convert_fusion.1 = (bf16[1024,2048]{1,0:T(8,128)(2,1)S(1)}, f32[1024,2048]{1,0:T(8,128)}) fusion(f32[1024,2048]{1,0:T(8,128)} %fusion.82.gate_ref, bf16[1024,2048]{1,0:T(8,128)(2,1)} %copy-done.4, bf16[2048,2048]{1,0:T(8,128)(2,1)} %place_tiles.15.refs_3_), kind=kOutput, calls=%fused_computation.136 | convolution fusion | flops 8602517504 | bytes 33554432 | tf_op jit(solution)/shard_map/cond/branch_1_fun/dot_general | solution.py:270
  441.4 22.9 %collective-permute-done.71 = bf16[256,2048]{1,0:T(8,128)(2,1)S(1)} collective-permute-done((bf16[256,2048]{1,0:T(8,128)(2,1)S(1)}, bf16[256,2048]{1,0:T(8,128)(2,1)S(1)}, u32[]{:S(2)}, u32[]{:S(2)}) %collective-permute-start.71) | collective-permute-done | bytes 1048608 | tf_op jit(solution)/shard_map/cond/branch_1_fun/ppermute | solution.py:59
  471.7 22.8 %collective-permute-done.73.refs_2_ = bf16[256,2048]{1,0:T(8,128)(2,1)S(1)} collective-permute-done((bf16[256,2048]{1,0:T(8,128)(2,1)S(1)}, bf16[256,2048]{1,0:T(8,128)(2,1)S(1)}, u32[]{:S(2)}, u32[]{:S(2)}) %collective-permute-start.73) | collective-permute-done | bytes 1048608 | tf_op jit(solution)/shard_map/cond/branch_1_fun/ppermute | solution.py:59
  500.1 13.4 %product_tn.15.refs_0_ = bf16[2048,2048]{1,0:T(8,128)(2,1)} custom-call(bf16[1024,2048]{1,0:T(8,128)(2,1)} %copy-done.91, bf16[1024,2048]{1,0:T(8,128)(2,1)} %copy-done.3), custom_call_target="tpu_custom_call" | custom-call | tf_op jit(solution)/shard_map/cond/branch_1_fun/product_tn/pallas_call | solution.py:287
  520.5 18.5 %inner_back.3 = (bf16[1024,2048]{1,0:T(8,128)(2,1)}, bf16[1024,2048]{1,0:T(8,128)(2,1)}) custom-call(bf16[1024,2048]{1,0:T(8,128)(2,1)} %copy-done.3, bf16[2048,2048]{1,0:T(8,128)(2,1)} %place_tiles.14.w_ref, f32[1024,2048]{1,0:T(8,128)} %fusion.82.gate_ref, f32[1024,2048]{1,0:T(8,128)} %get-tuple-element.465.up_ref), custom_call_target="tpu_custom_call" | custom-call | tf_op jit(solution)/shard_map/cond/branch_1_fun/inner_back/pallas_call | solution.py:332
  539.0 13.3 %product_tn.16.refs_1_ = bf16[2048,2048]{1,0:T(8,128)(2,1)} custom-call(bf16[1024,2048]{1,0:T(8,128)(2,1)} %copy-done.4, bf16[1024,2048]{1,0:T(8,128)(2,1)} %get-tuple-element.258.b_ref.refs_1_), custom_call_target="tpu_custom_call" | custom-call | tf_op jit(solution)/shard_map/cond/branch_1_fun/product_tn/pallas_call | solution.py:287
  573.2 13.4 %product_tn.17.refs_2_ = bf16[2048,2048]{1,0:T(8,128)(2,1)} custom-call(bf16[1024,2048]{1,0:T(8,128)(2,1)} %copy-done.4, bf16[1024,2048]{1,0:T(8,128)(2,1)} %get-tuple-element.257.b_ref.refs_0_), custom_call_target="tpu_custom_call" | custom-call | tf_op jit(solution)/shard_map/cond/branch_1_fun/product_tn/pallas_call | solution.py:287
  586.6 24.0 %product_nt.9 = bf16[1024,2048]{1,0:T(8,128)(2,1)} custom-call(bf16[1024,2048]{1,0:T(8,128)(2,1)} %get-tuple-element.257.b_ref.refs_0_, bf16[1024,2048]{1,0:T(8,128)(2,1)} %get-tuple-element.258.b_ref.refs_1_, bf16[2048,2048]{1,0:T(8,128)(2,1)} %place_tiles.13.refs_2_, bf16[2048,2048]{1,0:T(8,128)(2,1)} %place_tiles.15.refs_3_), custom_call_target="tpu_custom_call" | custom-call | tf_op jit(solution)/shard_map/cond/branch_1_fun/product_nt/pallas_call | solution.py:308
  677.6 14.9 %collective-permute-done.80.refs_2_ = bf16[256,2048]{1,0:T(8,128)(2,1)S(1)} collective-permute-done((bf16[256,2048]{1,0:T(8,128)(2,1)S(1)}, bf16[256,2048]{1,0:T(8,128)(2,1)S(1)}, u32[]{:S(2)}, u32[]{:S(2)}) %collective-permute-start.80) | collective-permute-done | bytes 1048608 | tf_op jit(solution)/shard_map/cond/branch_1_fun/ppermute | solution.py:59
  704.4 17.7 %attention_back.3 = (f32[1024,512]{1,0:T(8,128)}, f32[1024,512]{1,0:T(8,128)}, bf16[1024,512]{1,0:T(8,128)(2,1)S(1)}) custom-call(s32[1]{0:T(128)} %get-tuple-element.213.len_ref, bf16[1024,512]{1,0:T(8,128)(2,1)S(1)} %copy-done.11, bf16[1024,512]{1,0:T(8,128)(2,1)S(1)} %copy-done.13, bf16[1024,512]{1,0:T(8,128)(2,1)S(1)} %copy-done.14, ...), custom_call_target="tpu_custom_call" | custom-call | tf_op jit(solution)/shard_map/cond/branch_1_fun/attention_back/pallas_call | solution.py:418
  792.5 14.0 %renew.19 = (f32[128,128,128]{2,1,0:T(8,128)}, f32[128,128,128]{2,1,0:T(8,128)}, f32[128,128,128]{2,1,0:T(8,128)}, f32[128,128,128]{2,1,0:T(8,128)}) custom-call(s32[128]{0:T(128)S(1)} %copy-done.126, bf16[28,128,128]{2,1,0:T(8,128)(2,1)S(1)} %copy-done.22, ...), custom_call_target="tpu_custom_call", output_to_operand_aliasing={{0}: (22, {}), {1}: (23, {}), {2}: (24, {}), {3}: (25, {})} | custom-call | tf_op jit(solution)/shard_map/cond/branch_1_fun/renew/pallas_call | solution.py:484
  832.2 12.2 %product_nt.11 = bf16[1024,2048]{1,0:T(8,128)(2,1)} custom-call(bf16[1024,1536]{1,0:T(8,128)(2,1)} %pad_maximum_fusion.7.b_ref.refs_0_, bf16[2048,1536]{1,0:T(8,128)(2,1)} %get-tuple-element.222.refs_1_), custom_call_target="tpu_custom_call" | custom-call | tf_op jit(solution)/shard_map/cond/branch_1_fun/product_nt/pallas_call | solution.py:308
  844.4 26.5 %collective-permute-done.90 = bf16[49,128,128]{2,1,0:T(8,128)(2,1)S(1)} collective-permute-done((bf16[49,128,128]{2,1,0:T(8,128)(2,1)S(1)}, bf16[49,128,128]{2,1,0:T(8,128)(2,1)S(1)}, u32[]{:S(2)}, u32[]{:S(2)}) %collective-permute-start.90) | collective-permute-done | bytes 1605664 | tf_op jit(solution)/shard_map/cond/branch_1_fun/ppermute | solution.py:41
  949.4 16.3 %collective-permute-done.97 = bf16[25,128,128]{2,1,0:T(8,128)(2,1)S(1)} collective-permute-done((bf16[25,128,128]{2,1,0:T(8,128)(2,1)S(1)}, bf16[25,128,128]{2,1,0:T(8,128)(2,1)S(1)}, u32[]{:S(2)}, u32[]{:S(2)}) %collective-permute-start.97) | collective-permute-done | bytes 819232 | tf_op jit(solution)/shard_map/cond/branch_1_fun/ppermute | solution.py:52
  (457 shorter events, 533.8 us)
Async XLA Ops:
  8.0 46.2 %all-gather.26.cloned.1.call-start = ((), (), s32[]{:S(2)}) async-start(), calls=%async_computation.24 | async-start | bytes 5242880 | tf_op jit(solution)/shard_map/all_gather | solution.py:552
  14.2 37.5 %collective-permute-start.104 = (bf16[48,128,128]{2,1,0:T(8,128)(2,1)S(1)}, bf16[48,128,128]{2,1,0:T(8,128)(2,1)}, u32[]{:S(2)}, u32[]{:S(2)}) collective-permute-start(bf16[48,128,128]{2,1,0:T(8,128)(2,1)S(1)} %sorted_tiles.4), channel_id=1, source_target_pairs={{0,4},{4,0},{8,12},{12,8},{16,20},{20,16},{24,28},{28,24},{1,5},{5... | collective-permute-start | bytes 4718600 | tf_op jit(solution)/shard_map/ppermute | solution.py:52
  17.2 37.0 %collective-permute-start.103 = (bf16[48,128,128]{2,1,0:T(8,128)(2,1)S(1)}, bf16[48,128,128]{2,1,0:T(8,128)(2,1)}, u32[]{:S(2)}, u32[]{:S(2)}) collective-permute-start(bf16[48,128,128]{2,1,0:T(8,128)(2,1)S(1)} %sorted_tiles.4), channel_id=1, source_target_pairs={{0,24},{4,28},{8,0},{12,4},{16,8},{20,12},{24,16},{28,20},{1,25},{... | collective-permute-start | bytes 4718600 | tf_op jit(solution)/shard_map/ppermute | solution.py:41
  59.8 175.9 %all-gather.18.cloned.1.call-start = ((), (), s32[]{:S(2)}) async-start(), calls=%async_computation.16 | async-start | bytes 5898240 | tf_op jit(solution)/shard_map/cond/branch_1_fun/all_gather | solution.py:44
  59.8 37.2 %collective-permute-start.52 = (bf16[48,128,128]{2,1,0:T(8,128)(2,1)}, bf16[48,128,128]{2,1,0:T(8,128)(2,1)S(1)}, u32[]{:S(2)}, u32[]{:S(2)}) collective-permute-start(bf16[48,128,128]{2,1,0:T(8,128)(2,1)} %get-tuple-element.219.refs_2_), channel_id=1, source_target_pairs={{0,24},{4,28},{8,0},{12,4},{16,8},{20,12},{24,16},{28,20},{1,25},{... | collective-permute-start | bytes 4718600 | tf_op jit(solution)/shard_map/cond/branch_1_fun/ppermute | solution.py:41
  136.2 177.9 %all-gather.20.cloned.1.call-start = ((), (), s32[]{:S(2)}) async-start(), calls=%async_computation.17 | async-start | bytes 4587520 | tf_op jit(solution)/shard_map/cond/branch_1_fun/all_gather | solution.py:44
  136.9 247.4 %all-gather.22.cloned.1.call-start = ((), (), s32[]{:S(2)}) async-start(), calls=%async_computation.18 | async-start | bytes 5242880 | tf_op jit(solution)/shard_map/cond/branch_1_fun/all_gather | solution.py:44
  197.0 42.8 %collective-permute-start.58 = (bf16[28,128,128]{2,1,0:T(8,128)(2,1)}, bf16[28,128,128]{2,1,0:T(8,128)(2,1)}, u32[]{:S(2)}, u32[]{:S(2)}) collective-permute-start(bf16[28,128,128]{2,1,0:T(8,128)(2,1)} %get-tuple-element.243), channel_id=1, source_target_pairs={{0,4},{4,0},{8,12},{12,8},{16,20},{20,16},{24,28},{28,24},{1,5},{5... | collective-permute-start | bytes 2752520 | tf_op jit(solution)/shard_map/cond/branch_1_fun/ppermute | solution.py:52
  247.1 217.7 %all-gather.24.cloned.1.call-start = ((), (), s32[]{:S(2)}) async-start(), calls=%async_computation.19 | async-start | bytes 5242880 | tf_op jit(solution)/shard_map/cond/branch_1_fun/all_gather | solution.py:583
  352.9 280.8 %reduce-scatter.17.cloned.1.call-start = ((), (), s32[]{:S(2)}) async-start(), calls=%async_computation.20 | async-start | bytes 2621440 | tf_op jit(solution)/shard_map/cond/branch_1_fun/reduce_scatter | solution.py:47
  518.8 48.1 %collective-permute-start.75 = (bf16[64,128,128]{2,1,0:T(8,128)(2,1)}, bf16[64,128,128]{2,1,0:T(8,128)(2,1)}, u32[]{:S(2)}, u32[]{:S(2)}) collective-permute-start(bf16[64,128,128]{2,1,0:T(8,128)(2,1)} %bitcast.432), channel_id=1, source_target_pairs={{0,4},{4,0},{8,12},{12,8},{16,20},{20,16},{24,28},{28,24},{1,5},{5... | collective-permute-start | bytes 6291464 | tf_op jit(solution)/shard_map/cond/branch_1_fun/ppermute | solution.py:52
  566.9 43.7 %collective-permute-start.76 = (bf16[56,128,128]{2,1,0:T(8,128)(2,1)}, bf16[56,128,128]{2,1,0:T(8,128)(2,1)}, u32[]{:S(2)}, u32[]{:S(2)}) collective-permute-start(bf16[56,128,128]{2,1,0:T(8,128)(2,1)} %bitcast.434), channel_id=1, source_target_pairs={{0,4},{4,0},{8,12},{12,8},{16,20},{20,16},{24,28},{28,24},{1,5},{5... | collective-permute-start | bytes 5505032 | tf_op jit(solution)/shard_map/cond/branch_1_fun/ppermute | solution.py:52
  573.1 162.6 %reduce-scatter.19.cloned.1.call-start = ((), (), s32[]{:S(2)}) async-start(), calls=%async_computation.21 | async-start | bytes 4587520 | tf_op jit(solution)/shard_map/cond/branch_1_fun/reduce_scatter | solution.py:47
  621.6 42.1 %collective-permute-start.81 = (bf16[56,128,128]{2,1,0:T(8,128)(2,1)}, bf16[56,128,128]{2,1,0:T(8,128)(2,1)}, u32[]{:S(2)}, u32[]{:S(2)}) collective-permute-start(bf16[56,128,128]{2,1,0:T(8,128)(2,1)} %bitcast.92), channel_id=1, source_target_pairs={{0,4},{4,0},{8,12},{12,8},{16,20},{20,16},{24,28},{28,24},{1,5},{5... | collective-permute-start | bytes 5505032 | tf_op jit(solution)/shard_map/cond/branch_1_fun/ppermute | solution.py:52
  668.2 118.3 %reduce-scatter.21.cloned.1.call-start = ((), (), s32[]{:S(2)}) async-start(), calls=%async_computation.22 | async-start | bytes 2949120 | tf_op jit(solution)/shard_map/cond/branch_1_fun/reduce_scatter | solution.py:47
  668.2 54.9 %collective-permute-start.83 = (bf16[72,128,128]{2,1,0:T(8,128)(2,1)}, bf16[72,128,128]{2,1,0:T(8,128)(2,1)S(1)}, u32[]{:S(2)}, u32[]{:S(2)}) collective-permute-start(bf16[72,128,128]{2,1,0:T(8,128)(2,1)} %bitcast.429), channel_id=1, source_target_pairs={{0,4},{4,0},{8,12},{12,8},{16,20},{20,16},{24,28},{28,24},{1,5},{5... | collective-permute-start | bytes 7077896 | tf_op jit(solution)/shard_map/cond/branch_1_fun/ppermute | solution.py:52
  726.0 144.9 %reduce-scatter.23.cloned.1.call-start = ((), (), s32[]{:S(2)}) async-start(), calls=%async_computation.23 | async-start | bytes 2949120 | tf_op jit(solution)/shard_map/cond/branch_1_fun/reduce_scatter | solution.py:47
  726.2 60.3 %collective-permute-start.84 = (bf16[72,128,128]{2,1,0:T(8,128)(2,1)}, bf16[72,128,128]{2,1,0:T(8,128)(2,1)}, u32[]{:S(2)}, u32[]{:S(2)}) collective-permute-start(bf16[72,128,128]{2,1,0:T(8,128)(2,1)} %bitcast.428), channel_id=1, source_target_pairs={{0,4},{4,0},{8,12},{12,8},{16,20},{20,16},{24,28},{28,24},{1,5},{5... | collective-permute-start | bytes 7077896 | tf_op jit(solution)/shard_map/cond/branch_1_fun/ppermute | solution.py:52
  790.9 36.9 %collective-permute-start.89 = (bf16[49,128,128]{2,1,0:T(8,128)(2,1)}, bf16[49,128,128]{2,1,0:T(8,128)(2,1)S(1)}, u32[]{:S(2)}, u32[]{:S(2)}) collective-permute-start(bf16[49,128,128]{2,1,0:T(8,128)(2,1)} %bitcast.436), channel_id=1, source_target_pairs={{0,4},{4,0},{8,12},{12,8},{16,20},{20,16},{24,28},{28,24},{1,5},{5... | collective-permute-start | bytes 4816904 | tf_op jit(solution)/shard_map/cond/branch_1_fun/ppermute | solution.py:52
  828.6 42.3 %collective-permute-start.90 = (bf16[49,128,128]{2,1,0:T(8,128)(2,1)S(1)}, bf16[49,128,128]{2,1,0:T(8,128)(2,1)S(1)}, u32[]{:S(2)}, u32[]{:S(2)}) collective-permute-start(bf16[49,128,128]{2,1,0:T(8,128)(2,1)S(1)} %fusion.45), channel_id=1, source_target_pairs={{0,24},{4,28},{8,0},{12,4},{16,8},{20,12},{24,16},{28,20},{1,25},{... | collective-permute-start | bytes 4816904 | tf_op jit(solution)/shard_map/cond/branch_1_fun/ppermute | solution.py:41
  830.6 40.2 %collective-permute-start.85 = (bf16[49,128,128]{2,1,0:T(8,128)(2,1)}, bf16[49,128,128]{2,1,0:T(8,128)(2,1)S(1)}, u32[]{:S(2)}, u32[]{:S(2)}) collective-permute-start(bf16[49,128,128]{2,1,0:T(8,128)(2,1)} %bitcast.99), channel_id=1, source_target_pairs={{0,4},{4,0},{8,12},{12,8},{16,20},{20,16},{24,28},{28,24},{1,5},{5... | collective-permute-start | bytes 4816904 | tf_op jit(solution)/shard_map/cond/branch_1_fun/ppermute | solution.py:52
  874.5 56.2 %collective-permute-start.98 = (bf16[49,128,128]{2,1,0:T(8,128)(2,1)}, bf16[49,128,128]{2,1,0:T(8,128)(2,1)}, u32[]{:S(2)}, u32[]{:S(2)}) collective-permute-start(bf16[49,128,128]{2,1,0:T(8,128)(2,1)} %fusion.44), channel_id=1, source_target_pairs={{0,24},{4,28},{8,0},{12,4},{16,8},{20,12},{24,16},{28,20},{1,25},{... | collective-permute-start | bytes 4816904 | tf_op jit(solution)/shard_map/cond/branch_1_fun/ppermute | solution.py:41
  878.8 58.5 %collective-permute-start.91 = (bf16[2,256,2048]{2,1,0:T(8,128)(2,1)}, bf16[2,256,2048]{2,1,0:T(8,128)(2,1)S(1)}, u32[]{:S(2)}, u32[]{:S(2)}) collective-permute-start(bf16[2,256,2048]{2,1,0:T(8,128)(2,1)} %dynamic-slice_bitcast_fusion.8), channel_id=1, source_target_pairs={{0,1},{1,0},{2,3},{3,2},{4,5},{5,4},{6,7},{7,6},{8,9},{9,8},{10,11... | collective-permute-start | bytes 6291464 | tf_op jit(solution)/shard_map/cond/branch_1_fun/ppermute | solution.py:55
  892.9 36.0 %collective-permute-start.96 = (bf16[25,128,128]{2,1,0:T(8,128)(2,1)}, bf16[25,128,128]{2,1,0:T(8,128)(2,1)S(1)}, u32[]{:S(2)}, u32[]{:S(2)}) collective-permute-start(bf16[25,128,128]{2,1,0:T(8,128)(2,1)} %slice.204), channel_id=1, source_target_pairs={{0,4},{4,0},{8,12},{12,8},{16,20},{20,16},{24,28},{28,24},{1,5},{5... | collective-permute-start | bytes 2457608 | tf_op jit(solution)/shard_map/cond/branch_1_fun/ppermute | solution.py:52
  (134 other events, 2226.5 us)
Sparse Core Ops, SparseCore 0:
  10.4 37.3 all-gather.25
  136.3 89.3 all-gather.17
  227.4 70.5 all-gather.19
  299.5 79.3 all-gather.21
  380.4 33.0 all-gather.23
  573.2 43.9 reduce-scatter.16
  668.3 67.4 reduce-scatter.18
  738.1 48.3 reduce-scatter.20
  791.0 52.0 reduce-scatter.22

commit v3 on v2

--- a/solution.py
+++ b/solution.py
@@ -810,15 +810,13 @@
         pins = ()
         if event == 0:
             input_part = product_nt((after(d_qkv, total), w_qkv))
-            pins = (input_part, total_2b)
+            outs = renew(after(total_2b, input_part), perm, edge_a, held, outs)
+            fetched = fetch(after(perm, outs[0]), edge_a, held)
+            pins = (input_part, outs[0], fetched)
         if event == links.nz - 3:
             total_at_1 = total
     halves = ((0, mid), (mid, edge_a + 1))
     last_rings = []
-    outs = renew(total_2b, perm, edge_a, held, outs)
-    to_send[-2] = after(to_send[-2], outs[0])
-    fetched = fetch(after(perm, total), edge_a, held)
-    to_send[-1] = after(to_send[-1], fetched)
     for lo, hi in halves:
         got = links.swap_x(after(to_send[-2][lo:hi], x_done[-2]))
         x_done.append(got)

time: 1020 us -> 1000 us (0.980)
    ppermute x7, waiting for transfers between devices: 98.3 us -> 68.2 us  [ring(): return lax.ppermute(value, 'dp', pairs)]
    ppermute x24, waiting for transfers between devices: 214 us -> 236 us  [swap_x(): return lax.ppermute(value, 'dp', [(i, i ^ 1) for i in range(self.n_dp)])]
    cond x179 -> x175, local copies, waits for them, and re-layouts: 21.4 us -> 21 us
  transfers between devices with their start and end apart: 63 -> 63, of which waited for: 35 -> 34; matrix products, arithmetic and copies ran while one was open for 12% -> 12% of each run, Pallas kernels for 29% -> 30%
where the time goes in v3:
time: 1000 us; the launch traced here: 991 us
  waiting for transfers between devices  407 us (41%)
  Pallas kernels  316 us (32%)
  other arithmetic  72.3 us (7%)
  starting transfers between devices  59.5 us (6%)
  matrix products  48.8 us (5%)
  local copies, waits for them, and re-layouts  39 us (4%)
  blocking collectives  23.3 us (2%)
  between operations  17.2 us (2%)
    ppermute x24, waiting for transfers between devices, swap_x(): return lax.ppermute(value, 'dp', [(i, i ^ 1) for i in range(self.n_dp)])  236 us
    ppermute x7, waiting for transfers between devices, shift_y(): return lax.ppermute(value, 'tensor', pairs)  78.6 us
    ppermute x7, waiting for transfers between devices, ring(): return lax.ppermute(value, 'dp', pairs)  68.2 us
    pallas_call x6, Pallas kernels, renew(): pl.pallas_call(kernel, grid_spec=pltpu.PrefetchScalarGridSpec(num_scalar_...  59.4 us
    pallas_call x5, Pallas kernels, product_tn(): pl.pallas_call(kernel, grid=(m // step,), in_specs=[pl.BlockSpec((rows, s...  56.7 us
    dot_general x5, matrix products, dot_nn(): lax.dot_general(a, b, (((1,), (0,)), ((), ())), preferred_element_type=f32)  48.8 us
    pallas_call x3, Pallas kernels, product_nt(): pl.pallas_call(kernel, grid=(n // step,), in_specs=[kept(a.shape) for a,...  41.6 us
    pallas_call x6, Pallas kernels, pick_tiles(): pl.pallas_call(kernel, grid_spec=pltpu.PrefetchScalarGridSpec(num_scalar_...  38 us
  transfers between devices with their start and end apart: 63, of which 34 were waited for; matrix products, arithmetic and copies ran while one was open for 12% of the time, Pallas kernels for 30%

profile of v3, /device:TPU:0, one launch (start us, length us, event | category | flops | bytes accessed | tf_op | source)
XLA Modules:
  0.0 990.5 jit_solution(18066174395163761627)
XLA Ops:
  54.2 928.7 %conditional.1 = (bf16[1024,512]{1,0:T(8,128)(2,1)}, bf16[1024,512]{1,0:T(8,128)(2,1)}, f32[1,128,128,128]{3,2,1,0:T(8,128)}, f32[1,128,128,128]{3,2,1,0:T(8,128...) conditional(s32[]{:T(128)} %convert_element_type.588, ...), branch_computations={%region_6.25_spmd, %region_25.44_spmd} | conditional | flops 34508578816 | bytes 1215728384 | solution.py:923
  64.8 32.2 %collective-permute-done.52.refs_4_ = bf16[48,128,128]{2,1,0:T(8,128)(2,1)S(1)} collective-permute-done((bf16[48,128,128]{2,1,0:T(8,128)(2,1)}, bf16[48,128,128]{2,1,0:T(8,128)(2,1)S(1)}, u32[]{:S(2)}, u32[]{:S(2)}) %collective-permute-start.52) | collective-permute-done | bytes 1572896 | tf_op jit(solution)/shard_map/cond/branch_1_fun/ppermute | solution.py:41
  101.8 31.1 %collective-permute-done.54.refs_6_ = bf16[48,128,128]{2,1,0:T(8,128)(2,1)S(1)} collective-permute-done((bf16[48,128,128]{2,1,0:T(8,128)(2,1)S(1)}, bf16[48,128,128]{2,1,0:T(8,128)(2,1)S(1)}, u32[]{:S(2)}, u32[]{:S(2)}) %collective-permute-start.54) | collective-permute-done | bytes 1572896 | tf_op jit(solution)/shard_map/cond/branch_1_fun/ppermute | solution.py:41
  137.0 33.9 %collective-permute-done.55.refs_7_ = bf16[48,128,128]{2,1,0:T(8,128)(2,1)} collective-permute-done((bf16[48,128,128]{2,1,0:T(8,128)(2,1)}, bf16[48,128,128]{2,1,0:T(8,128)(2,1)}, u32[]{:S(2)}, u32[]{:S(2)}) %collective-permute-start.55) | collective-permute-done | bytes 1572896 | tf_op jit(solution)/shard_map/cond/branch_1_fun/ppermute | solution.py:52
  182.0 15.0 %collective-permute-done.56.refs_9_ = bf16[36,128,128]{2,1,0:T(8,128)(2,1)} collective-permute-done((bf16[36,128,128]{2,1,0:T(8,128)(2,1)}, bf16[36,128,128]{2,1,0:T(8,128)(2,1)}, u32[]{:S(2)}, u32[]{:S(2)}) %collective-permute-start.56) | collective-permute-done | bytes 1179680 | tf_op jit(solution)/shard_map/cond/branch_1_fun/ppermute | solution.py:52
  217.4 16.2 %attention.3 = (bf16[1024,512]{1,0:T(8,128)(2,1)S(1)}, bf16[1024,512]{1,0:T(8,128)(2,1)S(1)}, bf16[1024,512]{1,0:T(8,128)(2,1)S(1)}, bf16[1024,512]{1,0:T(8,128)(2,1)}) custom-call(s32[1]{0:T(128)} %get-tuple-element.212.len_ref, f32[1024,1536]{1,0:T(8,128)} %copy-done.32, f32[1024,1536]{1,0:T(8,128)} %copy-done.32, f32[1024,1536]{1,0:T(8,128)} %copy-done.32, ...), custom_call_target="tpu_custom_call" | custom-call | tf_op jit(solution)/shard_map/cond/branch_1_fun/attention/pallas_call | solution.py:376
  248.7 27.0 %collective-permute-done.64.refs_10_ = bf16[36,128,128]{2,1,0:T(8,128)(2,1)S(1)} collective-permute-done((bf16[36,128,128]{2,1,0:T(8,128)(2,1)}, bf16[36,128,128]{2,1,0:T(8,128)(2,1)S(1)}, u32[]{:S(2)}, u32[]{:S(2)}) %collective-permute-start.64) | collective-permute-done | bytes 1179680 | tf_op jit(solution)/shard_map/cond/branch_1_fun/ppermute | solution.py:52
  284.3 19.5 %collective-permute-done.65.refs_11_ = bf16[36,128,128]{2,1,0:T(8,128)(2,1)} collective-permute-done((bf16[36,128,128]{2,1,0:T(8,128)(2,1)}, bf16[36,128,128]{2,1,0:T(8,128)(2,1)}, u32[]{:S(2)}, u32[]{:S(2)}) %collective-permute-start.65) | collective-permute-done | bytes 1179680 | tf_op jit(solution)/shard_map/cond/branch_1_fun/ppermute | solution.py:52
  317.4 13.6 %collective-permute-done.66.refs_12_ = bf16[36,128,128]{2,1,0:T(8,128)(2,1)} collective-permute-done((bf16[36,128,128]{2,1,0:T(8,128)(2,1)}, bf16[36,128,128]{2,1,0:T(8,128)(2,1)}, u32[]{:S(2)}, u32[]{:S(2)}) %collective-permute-start.66) | collective-permute-done | bytes 1179680 | tf_op jit(solution)/shard_map/cond/branch_1_fun/ppermute | solution.py:52
  336.4 14.9 %collective-permute-done.67.refs_15_ = bf16[28,128,128]{2,1,0:T(8,128)(2,1)} collective-permute-done((bf16[28,128,128]{2,1,0:T(8,128)(2,1)S(1)}, bf16[28,128,128]{2,1,0:T(8,128)(2,1)}, u32[]{:S(2)}, u32[]{:S(2)}) %collective-permute-start.67) | collective-permute-done | bytes 917536 | tf_op jit(solution)/shard_map/cond/branch_1_fun/ppermute | solution.py:52
  408.1 16.4 %multiply_convert_fusion.1 = (bf16[1024,2048]{1,0:T(8,128)(2,1)S(1)}, f32[1024,2048]{1,0:T(8,128)}) fusion(f32[1024,2048]{1,0:T(8,128)} %fusion.82.gate_ref, bf16[1024,2048]{1,0:T(8,128)(2,1)} %copy-done.4, bf16[2048,2048]{1,0:T(8,128)(2,1)} %place_tiles.15.refs_3_), kind=kOutput, calls=%fused_computation.140 | convolution fusion | flops 8602517504 | bytes 33554432 | tf_op jit(solution)/shard_map/cond/branch_1_fun/dot_general | solution.py:270
  441.4 22.9 %collective-permute-done.71 = bf16[256,2048]{1,0:T(8,128)(2,1)S(1)} collective-permute-done((bf16[256,2048]{1,0:T(8,128)(2,1)S(1)}, bf16[256,2048]{1,0:T(8,128)(2,1)S(1)}, u32[]{:S(2)}, u32[]{:S(2)}) %collective-permute-start.71) | collective-permute-done | bytes 1048608 | tf_op jit(solution)/shard_map/cond/branch_1_fun/ppermute | solution.py:59
  471.8 22.7 %collective-permute-done.73.refs_2_ = bf16[256,2048]{1,0:T(8,128)(2,1)S(1)} collective-permute-done((bf16[256,2048]{1,0:T(8,128)(2,1)S(1)}, bf16[256,2048]{1,0:T(8,128)(2,1)S(1)}, u32[]{:S(2)}, u32[]{:S(2)}) %collective-permute-start.73) | collective-permute-done | bytes 1048608 | tf_op jit(solution)/shard_map/cond/branch_1_fun/ppermute | solution.py:59
  500.0 13.3 %product_tn.15.refs_0_ = bf16[2048,2048]{1,0:T(8,128)(2,1)} custom-call(bf16[1024,2048]{1,0:T(8,128)(2,1)} %copy-done.88, bf16[1024,2048]{1,0:T(8,128)(2,1)} %copy-done.3), custom_call_target="tpu_custom_call" | custom-call | tf_op jit(solution)/shard_map/cond/branch_1_fun/product_tn/pallas_call | solution.py:287
  520.3 18.5 %inner_back.3 = (bf16[1024,2048]{1,0:T(8,128)(2,1)}, bf16[1024,2048]{1,0:T(8,128)(2,1)}) custom-call(bf16[1024,2048]{1,0:T(8,128)(2,1)} %copy-done.3, bf16[2048,2048]{1,0:T(8,128)(2,1)} %place_tiles.14.w_ref, f32[1024,2048]{1,0:T(8,128)} %fusion.82.gate_ref, f32[1024,2048]{1,0:T(8,128)} %get-tuple-element.463.up_ref), custom_call_target="tpu_custom_call" | custom-call | tf_op jit(solution)/shard_map/cond/branch_1_fun/inner_back/pallas_call | solution.py:332
  538.8 13.4 %product_tn.16.refs_1_ = bf16[2048,2048]{1,0:T(8,128)(2,1)} custom-call(bf16[1024,2048]{1,0:T(8,128)(2,1)} %copy-done.4, bf16[1024,2048]{1,0:T(8,128)(2,1)} %get-tuple-element.257.b_ref.refs_1_), custom_call_target="tpu_custom_call" | custom-call | tf_op jit(solution)/shard_map/cond/branch_1_fun/product_tn/pallas_call | solution.py:287
  573.0 13.4 %product_tn.17.refs_2_ = bf16[2048,2048]{1,0:T(8,128)(2,1)} custom-call(bf16[1024,2048]{1,0:T(8,128)(2,1)} %copy-done.4, bf16[1024,2048]{1,0:T(8,128)(2,1)} %get-tuple-element.256.b_ref.refs_0_), custom_call_target="tpu_custom_call" | custom-call | tf_op jit(solution)/shard_map/cond/branch_1_fun/product_tn/pallas_call | solution.py:287
  586.4 24.0 %product_nt.9 = bf16[1024,2048]{1,0:T(8,128)(2,1)} custom-call(bf16[1024,2048]{1,0:T(8,128)(2,1)} %get-tuple-element.256.b_ref.refs_0_, bf16[1024,2048]{1,0:T(8,128)(2,1)} %get-tuple-element.257.b_ref.refs_1_, bf16[2048,2048]{1,0:T(8,128)(2,1)} %place_tiles.13.refs_2_, bf16[2048,2048]{1,0:T(8,128)(2,1)} %place_tiles.15.refs_3_), custom_call_target="tpu_custom_call" | custom-call | tf_op jit(solution)/shard_map/cond/branch_1_fun/product_nt/pallas_call | solution.py:308
  677.3 14.9 %collective-permute-done.80.refs_2_ = bf16[256,2048]{1,0:T(8,128)(2,1)S(1)} collective-permute-done((bf16[256,2048]{1,0:T(8,128)(2,1)S(1)}, bf16[256,2048]{1,0:T(8,128)(2,1)S(1)}, u32[]{:S(2)}, u32[]{:S(2)}) %collective-permute-start.80) | collective-permute-done | bytes 1048608 | tf_op jit(solution)/shard_map/cond/branch_1_fun/ppermute | solution.py:59
  704.2 17.7 %attention_back.3 = (f32[1024,512]{1,0:T(8,128)}, f32[1024,512]{1,0:T(8,128)}, bf16[1024,512]{1,0:T(8,128)(2,1)S(1)}) custom-call(s32[1]{0:T(128)} %get-tuple-element.212.len_ref, bf16[1024,512]{1,0:T(8,128)(2,1)S(1)} %copy-done.11, bf16[1024,512]{1,0:T(8,128)(2,1)S(1)} %copy-done.13, bf16[1024,512]{1,0:T(8,128)(2,1)S(1)} %copy-done.14, ...), custom_call_target="tpu_custom_call" | custom-call | tf_op jit(solution)/shard_map/cond/branch_1_fun/attention_back/pallas_call | solution.py:418
  792.2 14.0 %renew.19 = (f32[128,128,128]{2,1,0:T(8,128)}, f32[128,128,128]{2,1,0:T(8,128)}, f32[128,128,128]{2,1,0:T(8,128)}, f32[128,128,128]{2,1,0:T(8,128)}) custom-call(s32[128]{0:T(128)S(1)} %copy-done.121, bf16[28,128,128]{2,1,0:T(8,128)(2,1)S(1)} %copy-done.22, ...), custom_call_target="tpu_custom_call", output_to_operand_aliasing={{0}: (22, {}), {1}: (23, {}), {2}: (24, {}), {3}: (25, {})} | custom-call | tf_op jit(solution)/shard_map/cond/branch_1_fun/renew/pallas_call | solution.py:484
  887.0 28.2 %collective-permute-done.100 = bf16[24,128,128]{2,1,0:T(8,128)(2,1)S(1)} collective-permute-done((bf16[24,128,128]{2,1,0:T(8,128)(2,1)S(1)}, bf16[24,128,128]{2,1,0:T(8,128)(2,1)S(1)}, u32[]{:S(2)}, u32[]{:S(2)}) %collective-permute-start.100) | collective-permute-done | bytes 786464 | tf_op jit(solution)/shard_map/cond/branch_1_fun/ppermute | solution.py:52
  923.5 13.7 %collective-permute-done.101 = bf16[24,128,128]{2,1,0:T(8,128)(2,1)S(1)} collective-permute-done((bf16[24,128,128]{2,1,0:T(8,128)(2,1)S(1)}, bf16[24,128,128]{2,1,0:T(8,128)(2,1)S(1)}, u32[]{:S(2)}, u32[]{:S(2)}) %collective-permute-start.101) | collective-permute-done | bytes 786464 | tf_op jit(solution)/shard_map/cond/branch_1_fun/ppermute | solution.py:52
  937.2 14.7 %collective-permute-done.97 = bf16[25,128,128]{2,1,0:T(8,128)(2,1)S(1)} collective-permute-done((bf16[25,128,128]{2,1,0:T(8,128)(2,1)S(1)}, bf16[25,128,128]{2,1,0:T(8,128)(2,1)S(1)}, u32[]{:S(2)}, u32[]{:S(2)}) %collective-permute-start.97) | collective-permute-done | bytes 819232 | tf_op jit(solution)/shard_map/cond/branch_1_fun/ppermute | solution.py:52
  (453 shorter events, 514.5 us)
Async XLA Ops:
  8.0 46.2 %all-gather.26.cloned.1.call-start = ((), (), s32[]{:S(2)}) async-start(), calls=%async_computation.24 | async-start | bytes 5242880 | tf_op jit(solution)/shard_map/all_gather | solution.py:552
  14.2 37.5 %collective-permute-start.104 = (bf16[48,128,128]{2,1,0:T(8,128)(2,1)S(1)}, bf16[48,128,128]{2,1,0:T(8,128)(2,1)}, u32[]{:S(2)}, u32[]{:S(2)}) collective-permute-start(bf16[48,128,128]{2,1,0:T(8,128)(2,1)S(1)} %sorted_tiles.4), channel_id=1, source_target_pairs={{0,4},{4,0},{8,12},{12,8},{16,20},{20,16},{24,28},{28,24},{1,5},{5... | collective-permute-start | bytes 4718600 | tf_op jit(solution)/shard_map/ppermute | solution.py:52
  17.2 37.0 %collective-permute-start.103 = (bf16[48,128,128]{2,1,0:T(8,128)(2,1)S(1)}, bf16[48,128,128]{2,1,0:T(8,128)(2,1)}, u32[]{:S(2)}, u32[]{:S(2)}) collective-permute-start(bf16[48,128,128]{2,1,0:T(8,128)(2,1)S(1)} %sorted_tiles.4), channel_id=1, source_target_pairs={{0,24},{4,28},{8,0},{12,4},{16,8},{20,12},{24,16},{28,20},{1,25},{... | collective-permute-start | bytes 4718600 | tf_op jit(solution)/shard_map/ppermute | solution.py:41
  59.8 175.8 %all-gather.18.cloned.1.call-start = ((), (), s32[]{:S(2)}) async-start(), calls=%async_computation.16 | async-start | bytes 5898240 | tf_op jit(solution)/shard_map/cond/branch_1_fun/all_gather | solution.py:44
  59.8 37.2 %collective-permute-start.52 = (bf16[48,128,128]{2,1,0:T(8,128)(2,1)}, bf16[48,128,128]{2,1,0:T(8,128)(2,1)S(1)}, u32[]{:S(2)}, u32[]{:S(2)}) collective-permute-start(bf16[48,128,128]{2,1,0:T(8,128)(2,1)} %get-tuple-element.218.refs_2_), channel_id=1, source_target_pairs={{0,24},{4,28},{8,0},{12,4},{16,8},{20,12},{24,16},{28,20},{1,25},{... | collective-permute-start | bytes 4718600 | tf_op jit(solution)/shard_map/cond/branch_1_fun/ppermute | solution.py:41
  136.2 177.9 %all-gather.20.cloned.1.call-start = ((), (), s32[]{:S(2)}) async-start(), calls=%async_computation.17 | async-start | bytes 4587520 | tf_op jit(solution)/shard_map/cond/branch_1_fun/all_gather | solution.py:44
  136.9 247.5 %all-gather.22.cloned.1.call-start = ((), (), s32[]{:S(2)}) async-start(), calls=%async_computation.18 | async-start | bytes 5242880 | tf_op jit(solution)/shard_map/cond/branch_1_fun/all_gather | solution.py:44
  197.0 42.7 %collective-permute-start.58 = (bf16[28,128,128]{2,1,0:T(8,128)(2,1)}, bf16[28,128,128]{2,1,0:T(8,128)(2,1)}, u32[]{:S(2)}, u32[]{:S(2)}) collective-permute-start(bf16[28,128,128]{2,1,0:T(8,128)(2,1)} %get-tuple-element.242), channel_id=1, source_target_pairs={{0,4},{4,0},{8,12},{12,8},{16,20},{20,16},{24,28},{28,24},{1,5},{5... | collective-permute-start | bytes 2752520 | tf_op jit(solution)/shard_map/cond/branch_1_fun/ppermute | solution.py:52
  247.1 217.7 %all-gather.24.cloned.1.call-start = ((), (), s32[]{:S(2)}) async-start(), calls=%async_computation.19 | async-start | bytes 5242880 | tf_op jit(solution)/shard_map/cond/branch_1_fun/all_gather | solution.py:583
  352.9 280.6 %reduce-scatter.17.cloned.1.call-start = ((), (), s32[]{:S(2)}) async-start(), calls=%async_computation.20 | async-start | bytes 2621440 | tf_op jit(solution)/shard_map/cond/branch_1_fun/reduce_scatter | solution.py:47
  518.6 48.0 %collective-permute-start.75 = (bf16[64,128,128]{2,1,0:T(8,128)(2,1)}, bf16[64,128,128]{2,1,0:T(8,128)(2,1)}, u32[]{:S(2)}, u32[]{:S(2)}) collective-permute-start(bf16[64,128,128]{2,1,0:T(8,128)(2,1)} %bitcast.436), channel_id=1, source_target_pairs={{0,4},{4,0},{8,12},{12,8},{16,20},{20,16},{24,28},{28,24},{1,5},{5... | collective-permute-start | bytes 6291464 | tf_op jit(solution)/shard_map/cond/branch_1_fun/ppermute | solution.py:52
  566.6 43.7 %collective-permute-start.76 = (bf16[56,128,128]{2,1,0:T(8,128)(2,1)}, bf16[56,128,128]{2,1,0:T(8,128)(2,1)}, u32[]{:S(2)}, u32[]{:S(2)}) collective-permute-start(bf16[56,128,128]{2,1,0:T(8,128)(2,1)} %bitcast.438), channel_id=1, source_target_pairs={{0,4},{4,0},{8,12},{12,8},{16,20},{20,16},{24,28},{28,24},{1,5},{5... | collective-permute-start | bytes 5505032 | tf_op jit(solution)/shard_map/cond/branch_1_fun/ppermute | solution.py:52
  572.9 162.6 %reduce-scatter.19.cloned.1.call-start = ((), (), s32[]{:S(2)}) async-start(), calls=%async_computation.21 | async-start | bytes 4587520 | tf_op jit(solution)/shard_map/cond/branch_1_fun/reduce_scatter | solution.py:47
  621.4 42.1 %collective-permute-start.81 = (bf16[56,128,128]{2,1,0:T(8,128)(2,1)}, bf16[56,128,128]{2,1,0:T(8,128)(2,1)}, u32[]{:S(2)}, u32[]{:S(2)}) collective-permute-start(bf16[56,128,128]{2,1,0:T(8,128)(2,1)} %bitcast.94), channel_id=1, source_target_pairs={{0,4},{4,0},{8,12},{12,8},{16,20},{20,16},{24,28},{28,24},{1,5},{5... | collective-permute-start | bytes 5505032 | tf_op jit(solution)/shard_map/cond/branch_1_fun/ppermute | solution.py:52
  667.9 118.4 %reduce-scatter.21.cloned.1.call-start = ((), (), s32[]{:S(2)}) async-start(), calls=%async_computation.22 | async-start | bytes 2949120 | tf_op jit(solution)/shard_map/cond/branch_1_fun/reduce_scatter | solution.py:47
  667.9 55.0 %collective-permute-start.83 = (bf16[72,128,128]{2,1,0:T(8,128)(2,1)}, bf16[72,128,128]{2,1,0:T(8,128)(2,1)S(1)}, u32[]{:S(2)}, u32[]{:S(2)}) collective-permute-start(bf16[72,128,128]{2,1,0:T(8,128)(2,1)} %bitcast.433), channel_id=1, source_target_pairs={{0,4},{4,0},{8,12},{12,8},{16,20},{20,16},{24,28},{28,24},{1,5},{5... | collective-permute-start | bytes 7077896 | tf_op jit(solution)/shard_map/cond/branch_1_fun/ppermute | solution.py:52
  725.8 123.7 %reduce-scatter.23.cloned.1.call-start = ((), (), s32[]{:S(2)}) async-start(), calls=%async_computation.23 | async-start | bytes 2949120 | tf_op jit(solution)/shard_map/cond/branch_1_fun/reduce_scatter | solution.py:47
  726.1 60.2 %collective-permute-start.84 = (bf16[72,128,128]{2,1,0:T(8,128)(2,1)}, bf16[72,128,128]{2,1,0:T(8,128)(2,1)}, u32[]{:S(2)}, u32[]{:S(2)}) collective-permute-start(bf16[72,128,128]{2,1,0:T(8,128)(2,1)} %bitcast.432), channel_id=1, source_target_pairs={{0,4},{4,0},{8,12},{12,8},{16,20},{20,16},{24,28},{28,24},{1,5},{5... | collective-permute-start | bytes 7077896 | tf_op jit(solution)/shard_map/cond/branch_1_fun/ppermute | solution.py:52
  790.6 36.9 %collective-permute-start.89 = (bf16[49,128,128]{2,1,0:T(8,128)(2,1)}, bf16[49,128,128]{2,1,0:T(8,128)(2,1)S(1)}, u32[]{:S(2)}, u32[]{:S(2)}) collective-permute-start(bf16[49,128,128]{2,1,0:T(8,128)(2,1)} %bitcast.439), channel_id=1, source_target_pairs={{0,4},{4,0},{8,12},{12,8},{16,20},{20,16},{24,28},{28,24},{1,5},{5... | collective-permute-start | bytes 4816904 | tf_op jit(solution)/shard_map/cond/branch_1_fun/ppermute | solution.py:52
  829.6 42.8 %collective-permute-start.90 = (bf16[49,128,128]{2,1,0:T(8,128)(2,1)}, bf16[49,128,128]{2,1,0:T(8,128)(2,1)}, u32[]{:S(2)}, u32[]{:S(2)}) collective-permute-start(bf16[49,128,128]{2,1,0:T(8,128)(2,1)} %fusion.45), channel_id=1, source_target_pairs={{0,24},{4,28},{8,0},{12,4},{16,8},{20,12},{24,16},{28,20},{1,25},{... | collective-permute-start | bytes 4816904 | tf_op jit(solution)/shard_map/cond/branch_1_fun/ppermute | solution.py:41
  831.6 40.8 %collective-permute-start.85 = (bf16[49,128,128]{2,1,0:T(8,128)(2,1)}, bf16[49,128,128]{2,1,0:T(8,128)(2,1)}, u32[]{:S(2)}, u32[]{:S(2)}) collective-permute-start(bf16[49,128,128]{2,1,0:T(8,128)(2,1)} %bitcast.101), channel_id=1, source_target_pairs={{0,4},{4,0},{8,12},{12,8},{16,20},{20,16},{24,28},{28,24},{1,5},{5... | collective-permute-start | bytes 4816904 | tf_op jit(solution)/shard_map/cond/branch_1_fun/ppermute | solution.py:52
  875.3 42.4 %collective-permute-start.98 = (bf16[49,128,128]{2,1,0:T(8,128)(2,1)S(1)}, bf16[49,128,128]{2,1,0:T(8,128)(2,1)S(1)}, u32[]{:S(2)}, u32[]{:S(2)}) collective-permute-start(bf16[49,128,128]{2,1,0:T(8,128)(2,1)S(1)} %fusion.44), channel_id=1, source_target_pairs={{0,24},{4,28},{8,0},{12,4},{16,8},{20,12},{24,16},{28,20},{1,25},{... | collective-permute-start | bytes 4816904 | tf_op jit(solution)/shard_map/cond/branch_1_fun/ppermute | solution.py:41
  877.5 43.3 %collective-permute-start.91 = (bf16[2,256,2048]{2,1,0:T(8,128)(2,1)S(1)}, bf16[2,256,2048]{2,1,0:T(8,128)(2,1)S(1)}, u32[]{:S(2)}, u32[]{:S(2)}) collective-permute-start(bf16[2,256,2048]{2,1,0:T(8,128)(2,1)S(1)} %dynamic-slice_bitcast_fusion.8), channel_id=1, source_target_pairs={{0,1},{1,0},{2,3},{3,2},{4,5},{5,4},{6,7},{7,6},{8,9},{9,8},{10,11... | collective-permute-start | bytes 6291464 | tf_op jit(solution)/shard_map/cond/branch_1_fun/ppermute | solution.py:55
  878.8 37.9 %collective-permute-start.96 = (bf16[25,128,128]{2,1,0:T(8,128)(2,1)S(1)}, bf16[25,128,128]{2,1,0:T(8,128)(2,1)S(1)}, u32[]{:S(2)}, u32[]{:S(2)}) collective-permute-start(bf16[25,128,128]{2,1,0:T(8,128)(2,1)S(1)} %slice_bitcast_fusion.7), channel_id=1, source_target_pairs={{0,4},{4,0},{8,12},{12,8},{16,20},{20,16},{24,28},{28,24},{1,5},{5... | collective-permute-start | bytes 2457608 | tf_op jit(solution)/shard_map/cond/branch_1_fun/ppermute | solution.py:52
  (132 other events, 2206.6 us)
Sparse Core Ops, SparseCore 0:
  10.4 37.3 all-gather.25
  136.3 89.4 all-gather.17
  227.4 70.5 all-gather.19
  299.5 79.3 all-gather.21
  380.4 33.0 all-gather.23
  573.0 43.9 reduce-scatter.16
  668.0 67.4 reduce-scatter.18
  737.8 48.3 reduce-scatter.20
  790.7 50.6 reduce-scatter.22
